TPU v7x, 128 devices: a whole 4x4x4 slice. The times are simulated.
128 devices in a mesh: fsdp: 16 (over x_lo, y, core), tp: 8 (over x_hi, z).
Axes of the slice: x: 4 (x_hi: 2, x_lo: 2; x = x_hi * 2 + x_lo), y: 4, z: 4, core: 2. Of those that a mesh axis runs over, the one named last changes fastest.
Arguments:
- master: float32 [8192, 10240], P(('fsdp', 'tp')), may hold values from -0.0625 to 0.0625
- moment: float32 [8192, 10240], P(('fsdp', 'tp')), may hold values from -0.02 to 0.02
- second: float32 [8192, 10240], P(('fsdp', 'tp')), may hold values from 1e-06 to 0.0001
- grad: bfloat16 [8192, 10240], P(('fsdp', 'tp')), may hold values from -0.019897461 to 0.019897461
- hidden: bfloat16 [64, 4, 8192], P('fsdp'), may hold values from -6 to 6
- cache: bfloat16 [64, 8, 2, 4096, 128], P('fsdp', 'tp'), may hold values from -400 to 400
- lengths: int32 [64], P('fsdp'), may hold values from 1 to 4096, as said below
- recorded: float32 [64, 4], P('fsdp'), may hold values from 5 to 10
- versions: int32 [64], P('fsdp'), may hold values from 0 to 3, as said below
Outputs:
- new_master: float32 [8192, 10240], P(('fsdp', 'tp'))
- attention: bfloat16 [64, 4, 8192], P('fsdp', None, 'tp')
- ratios: float32 [64, 4], P('fsdp')
- version_means: float32 [4], replicated
Inputs may be any that keep to these rules, and one draw needn't show every extreme that they name: `lengths`: every row has at least one live slot; some row fills all 4096 slots. `versions`: some version may be named by no row.
All inputs are finite; a program needn't handle non-finite values.
Results may differ from a plain program's by a relative error of at most 0.0059.
The roundings to bfloat16 on the way count: a program that leaves them out, or rounds other values in their place, can miss the bound.
Values may be sent and summed in bfloat16 or wider, within the bound.
No kernel may reach another device: no remote copies, remote signals or barrier semaphores. Data moves between devices by JAX's collectives and lax.ppermute only.
A program may use at most 128 MiB of HBM per device.

v0:
```python
import jax
import jax.numpy as jnp
from jax import lax
from jax.sharding import PartitionSpec as P

H = 64
HD = 128
CACHE = 4096
VERSIONS = 4


def adam_update(master, moment, second, grad):
    gradient = grad.astype(jnp.float32)
    fresh_moment = 0.9 * moment + 0.1 * gradient
    fresh_second = 0.95 * second + 0.05 * gradient * gradient
    corrected = fresh_moment / (1.0 - 0.9**10)
    spread = jnp.sqrt(fresh_second / (1.0 - 0.95**10)) + 1e-08
    return master - 0.005 * corrected / spread


def shards(master, moment, second, grad, hidden, cache, lengths, recorded, versions):
    new_master = adam_update(master, moment, second, grad)
    fresh = new_master.astype(jnp.bfloat16)
    local_weights = lax.all_to_all(fresh, "tp", split_axis=1, concat_axis=0, tiled=True)
    row_count = hidden.shape[0]
    step_count = hidden.shape[1]
    width = hidden.shape[2]
    columns = local_weights.shape[1]
    flat_rows = hidden.reshape(row_count * step_count, width)
    qkv = jnp.dot(
        flat_rows,
        lax.all_gather(local_weights, "fsdp", axis=0, tiled=True),
        preferred_element_type=jnp.float32,
    )
    local_kv = cache.shape[1]
    local_heads = columns // HD - 2 * local_kv
    group = local_heads // local_kv
    qkv = qkv.reshape(row_count, step_count, local_heads + 2 * local_kv, HD)
    queries = (
        qkv[:, :, :local_heads]
        .astype(jnp.bfloat16)
        .reshape(row_count, step_count, local_kv, group, HD)
    )
    new_keys = qkv[:, :, local_heads : local_heads + local_kv].astype(jnp.bfloat16)
    new_values = qkv[:, :, local_heads + local_kv :].astype(jnp.bfloat16)
    old_keys = cache[:, :, 0]
    old_values = cache[:, :, 1]
    scale = HD ** (-0.5)
    cache_scores = (
        jnp.einsum("rsgqd,rgcd->rsgqc", queries, old_keys, preferred_element_type=jnp.float32)
        * scale
    )
    slot_live = jnp.arange(CACHE, dtype=jnp.int32)[None, :] < lengths[:, None]
    cache_scores = jnp.where(slot_live[:, None, None, None, :], cache_scores, -1e30)
    new_scores = (
        jnp.einsum("rsgqd,rtgd->rsgqt", queries, new_keys, preferred_element_type=jnp.float32)
        * scale
    )
    causal = jnp.arange(step_count)[:, None] >= jnp.arange(step_count)[None, :]
    new_scores = jnp.where(causal[None, :, None, None, :], new_scores, -1e30)
    top = jnp.maximum(jnp.max(cache_scores, axis=-1), jnp.max(new_scores, axis=-1))
    cache_exp = jnp.exp(cache_scores - top[..., None])
    new_exp = jnp.exp(new_scores - top[..., None])
    total = jnp.sum(cache_exp, axis=-1) + jnp.sum(new_exp, axis=-1)
    lse = top + jnp.log(total)
    cache_probs = (cache_exp / total[..., None]).astype(jnp.bfloat16)
    new_probs = (new_exp / total[..., None]).astype(jnp.bfloat16)
    output = jnp.einsum(
        "rsgqc,rgcd->rsgqd", cache_probs, old_values, preferred_element_type=jnp.float32
    )
    output = output + jnp.einsum(
        "rsgqt,rtgd->rsgqd", new_probs, new_values, preferred_element_type=jnp.float32
    )
    attention = output.reshape(row_count, step_count, local_heads * HD).astype(jnp.bfloat16)
    head_total = jnp.sum(lse.reshape(row_count, step_count, local_heads), axis=-1)
    normalizer = lax.psum(head_total, "tp") / H
    ratios = jnp.exp(jnp.clip(normalizer - recorded, -2.0, 2.0))
    onehot = (versions[:, None] == jnp.arange(VERSIONS, dtype=jnp.int32)[None, :]).astype(
        jnp.float32
    )
    sums = jnp.sum(jnp.sum(ratios, axis=1)[:, None] * onehot, axis=0)
    counts = jnp.sum(onehot, axis=0) * step_count
    sums, counts = lax.psum((sums, counts), "fsdp")
    version_means = sums / jnp.maximum(counts, 1.0)
    return (new_master, attention, ratios, version_means)


def solution(mesh):
    in_specs = (
        P(("fsdp", "tp"), None),
        P(("fsdp", "tp"), None),
        P(("fsdp", "tp"), None),
        P(("fsdp", "tp"), None),
        P("fsdp", None, None),
        P("fsdp", "tp", None, None, None),
        P("fsdp"),
        P("fsdp", None),
        P("fsdp"),
    )
    out_specs = (P(("fsdp", "tp"), None), P("fsdp", None, "tp"), P("fsdp", None), P())
    return jax.shard_map(shards, mesh=mesh, in_specs=in_specs, out_specs=out_specs, check_vma=False)
```

profile of v0, /device:TPU:1, one launch (start us, length us, event | category | flops | bytes accessed | tf_op | source)
XLA Modules:
  0.0 228.5 jit_solution(1762166318476312850)
XLA Ops:
  7.2 0.0 all-gather.2.cloned.1.call-start
  7.2 7.0 %fusion.37 = (bf16[64,10240]{1,0:T(8,128)(2,1)S(1)}, f32[64,10240]{1,0:T(8,128)}) fusion(f32[64,10240]{1,0:T(8,128)} %param.9, f32[64,10240]{1,0:T(8,128)} %param.11, bf16[64,10240]{1,0:T(8,128)(2,1)} %param.12, f32[64,10240]{1,0:T(8,128)} %param.10), kind=kLoop, calls=%fused_computation.55 | loop fusion | flops 9175040 | bytes 13107200 | tf_op jit(solution)/shard_map/convert_element_type | solution.py:23
  14.2 0.1 copy.46
  14.3 0.0 copy-start
  14.3 0.0 copy-start.2
  14.3 26.8 %all_to_all.19 = bf16[64,8,1280]{2,0,1:T(8,128)(2,1)} all-to-all(bf16[64,8,1280]{2,0,1:T(8,128)(2,1)S(1)} %bitcast.79), channel_id=1, replica_groups=mesh['fsdp'=16,'tp'=8] {'tp'}, dimensions={1} | all-to-all | bytes 2621440 | tf_op jit(solution)/shard_map/all_to_all | solution.py:24
  41.1 0.0 all-gather.2.cloned.1.call-update
  41.1 0.0 copy-done
  41.1 0.1 reshape.134
  41.2 0.0 copy-done.2
  41.2 0.1 iota_compare_fusion
  41.3 111.0 %all-gather.2.cloned.1.call-done = bf16[8192,1280]{1,0:T(8,128)(2,1)} async-done(((bf16[512,1280]{1,0:T(8,128)(2,1)}), bf16[8192,1280]{1,0:T(8,128)(2,1)}) %all-gather.2.cloned.1.call-update) | async-done | bytes 20971536 | tf_op jit(solution)/shard_map/all_gather | solution.py:32
  152.3 8.4 %fusion.16 = bf16[16,1280]{1,0:T(8,128)(2,1)S(1)} fusion(bf16[16,8192]{1,0:T(8,128)(2,1)S(1)} %reshape.134, bf16[8192,1280]{1,0:T(8,128)(2,1)} %all-gather.2.cloned.1.call-done), kind=kOutput, calls=%fused_computation.20 | convolution fusion | flops 335564800 | bytes 21274624 | tf_op jit(solution)/shard_map/dot_general | solution.py:30
  160.8 0.3 fusion.41
  161.1 0.0 copy-start.1
  161.1 0.0 copy-start.3
  161.1 3.7 %fusion.40 = (f32[4,4,8]{2,1,0:T(4,128)S(1)}, f32[4,4,1,8,4096]{4,3,1,0,2:T(8,128)S(1)}) fusion(bf16[4,1,2,4096,128]{4,3,2,1,0:T(8,128)(2,1)} %param.14, bf16[4,4,10,128]{3,2,1,0:T(8,128)(2,1)S(1)} %reshape.142, pred[4,4096]{1,0:T(4,128)(4,1)S(1)} %iota_compare_fusion), kind=kOutput, calls=%fused_computation.57 | convolution fusion | flops 135790464 | bytes 6341120 | tf_op jit(solution)/shard_map/rsgqd,rgcd->rsgqc/dot_general | solution.py:50
  164.9 0.4 fusion.17
  165.3 0.1 add_reduce_fusion
  165.4 20.5 %psum.21 = f32[4,4]{1,0:T(4,128)S(1)} all-reduce(f32[4,4]{1,0:T(4,128)S(1)} %get-tuple-element.10), channel_id=1, replica_groups=mesh['fsdp'=16,'tp'=8] {'tp'}, use_global_device_ids=true, to_apply=%region_5.6 | all-reduce | flops 16 | bytes 128 | tf_op jit(solution)/shard_map/psum | solution.py:76
  186.0 0.0 copy-done.1
  186.0 0.7 fusion.36
  186.7 0.0 copy-done.3
  186.7 0.1 convert_reduce_fusion
  186.8 3.0 %fusion.18 = f32[4,128,4,8]{1,3,2,0:T(8,128)S(1)} fusion(bf16[4,1,2,4096,128]{4,3,2,1,0:T(8,128)(2,1)} %param.14, f32[4,4,1,8,4096]{4,3,1,0,2:T(8,128)S(1)} %get-tuple-element.17, f32[4,4,8]{2,1,0:T(4,128)S(1)} %get-tuple-element.11, f32[4,4,8]{2,1,0:T(4,128)S(1)} %max.20), kind=kOutput, calls=%fused_computation.25 | convolution fusion | flops 135790592 | bytes 6358016 | tf_op jit(solution)/shard_map/rsgqc,rgcd->rsgqd/dot_general | solution.py:68
  189.8 0.2 fusion.22
  190.0 0.6 convert_element_type.37
  190.6 30.5 %all-reduce = (f32[4]{0:T(128)S(1)}, f32[4]{0:T(128)S(1)}) all-reduce(f32[4]{0:T(128)S(1)} %get-tuple-element.5, f32[4]{0:T(128)S(1)} %broadcast_multiply_fusion), channel_id=1, replica_groups=mesh['fsdp'=16,'tp'=8] {'fsdp'}, use_global_device_ids=true, to_apply=%region_8.9 | all-reduce | flops 8 | bytes 64 | tf_op jit(solution)/shard_map/psum | solution.py:83
  221.1 0.5 maximum_divide_fusion
  (6 shorter events, 0.1 us)
Async XLA Ops:
  7.2 145.1 %all-gather.2.cloned.1.call-start = ((), (), s32[]{:S(2)}) async-start(), calls=%async_computation.1 | async-start | bytes 22282240 | tf_op jit(solution)/shard_map/all_gather | solution.py:32
  14.3 26.8 %copy-start = (bf16[4,4,8192]{2,1,0:T(4,128)(2,1)S(1)}, bf16[4,4,8192]{2,1,0:T(4,128)(2,1)}, u32[]{:S(2)}) copy-start(bf16[4,4,8192]{2,1,0:T(4,128)(2,1)} %param.13) | copy-start | bytes 786436
  14.3 26.9 %copy-start.2 = (s32[4]{0:T(128)S(1)}, s32[4]{0:T(128)}, u32[]{:S(2)}) copy-start(s32[4]{0:T(128)} %param.15) | copy-start | bytes 52
  161.1 24.9 %copy-start.1 = (f32[4,4]{1,0:T(4,128)S(1)}, f32[4,4]{1,0:T(4,128)}, u32[]{:S(2)}) copy-start(f32[4,4]{1,0:T(4,128)} %param.16) | copy-start | bytes 196
  161.1 25.6 %copy-start.3 = (s32[4]{0:T(128)S(1)}, s32[4]{0:T(128)}, u32[]{:S(2)}) copy-start(s32[4]{0:T(128)} %param.17) | copy-start | bytes 52
Sparse Core Ops, SparseCore 0:
  41.2 110.9 all-gather.1
where the time goes:
time: 229 us; the launch traced here: 228 us
  waiting for transfers between devices  111 us (48%)
  blocking collectives  77.8 us (34%)
  matrix products  15.7 us (7%)
  between operations  14.1 us (6%)
  other arithmetic  9.01 us (4%)
    all_gather x1, waiting for transfers between devices, shards(): lax.all_gather(local_weights, 'fsdp', axis=0, tiled=True)  111 us
    psum x1, blocking collectives, shards(): sums, counts = lax.psum((sums, counts), 'fsdp')  30.5 us
    all_to_all x1, blocking collectives, shards(): lax.all_to_all(fresh, 'tp', split_axis=1, concat_axis=0, tiled=True)  26.8 us
    psum x1, blocking collectives, shards(): normalizer = lax.psum(head_total, 'tp') / H  20.5 us
    dot_general x1, matrix products, shards(): jnp.dot(flat_rows, lax.all_gather(local_weights, 'fsdp', axis=0, tiled=Tr...  8.43 us
    convert_element_type x1, other arithmetic, shards(): fresh = new_master.astype(jnp.bfloat16)  7.01 us
  transfers between devices with their start and end apart: 1, of which 1 were waited for; matrix products, arithmetic and copies ran while one was open for 0% of the time, Pallas kernels for 0%

commit v1 on v0

v1 whole, which is shorter than its diff:
```python
import functools

import jax
import jax.numpy as jnp
from jax import lax
from jax.experimental import pallas as pl
from jax.experimental.pallas import tpu as pltpu
from jax.sharding import PartitionSpec as P

H = 64
HD = 128
VERSIONS = 4
F32 = jnp.float32
BF16 = jnp.bfloat16


def adam_kernel(master_ref, moment_ref, second_ref, grad_ref, new_ref, weight_ref):
    gradient = grad_ref[...].astype(F32)
    fresh_moment = 0.9 * moment_ref[...] + 0.1 * gradient
    fresh_second = 0.95 * second_ref[...] + 0.05 * gradient * gradient
    spread = jnp.sqrt(fresh_second / (1.0 - 0.95**10)) + 1e-08
    fresh = master_ref[...] - (0.005 / (1.0 - 0.9**10)) * fresh_moment / spread
    new_ref[...] = fresh
    weight_ref[0] = fresh.astype(BF16)


def adam(master, moment, second, grad, n_tp):
    rows, columns = master.shape
    width = columns // n_tp
    block = pl.BlockSpec((rows, width), lambda i: (0, i))
    return pl.pallas_call(
        adam_kernel,
        grid=(n_tp,),
        in_specs=[block] * 4,
        out_specs=[block, pl.BlockSpec((1, rows, width), lambda i: (i, 0, 0))],
        out_shape=[
            jax.ShapeDtypeStruct((rows, columns), F32),
            jax.ShapeDtypeStruct((n_tp, rows, width), BF16),
        ],
        compiler_params=pltpu.CompilerParams(vmem_limit_bytes=24 << 20),
        cost_estimate=pl.CostEstimate(
            flops=12 * rows * columns, bytes_accessed=20 * rows * columns, transcendentals=0
        ),
        name="adam",
    )(master, moment, second, grad)


def attention_kernel(heads, steps, copies, lengths_ref, parts_ref, cache_ref, out_ref, lse_ref, qkv):
    row = pl.program_id(0)

    @pl.when(row == 0)
    def _():
        total = parts_ref[0]
        for i in range(1, parts_ref.shape[0]):
            total = total + parts_ref[i]
        qkv[...] = total.reshape(qkv.shape)
        lse_ref[...] = jnp.zeros_like(lse_ref)

    mine = qkv[row]
    queries = jnp.concatenate(
        [mine[:, h * HD : (h + 1) * HD] for h in range(heads)], axis=0
    ).astype(BF16)
    new_keys = mine[:, heads * HD : (heads + 1) * HD].astype(BF16)
    new_values = mine[:, (heads + 1) * HD :].astype(BF16)
    scale = HD ** (-0.5)
    contract = (((1,), (1,)), ((), ()))
    scores = lax.dot_general(queries, cache_ref[0, 0, 0], contract, preferred_element_type=F32) * scale
    slot = lax.broadcasted_iota(jnp.int32, scores.shape, 1)
    scores = jnp.where(slot < lengths_ref[row], scores, -1e30)
    fresh = lax.dot_general(queries, new_keys, contract, preferred_element_type=F32) * scale
    step = lax.broadcasted_iota(jnp.int32, fresh.shape, 0) % steps
    later = lax.broadcasted_iota(jnp.int32, fresh.shape, 1)
    fresh = jnp.where(later <= step, fresh, -1e30)
    top = jnp.maximum(
        jnp.max(scores, axis=1, keepdims=True), jnp.max(fresh, axis=1, keepdims=True)
    )
    scores = jnp.exp(scores - top)
    fresh = jnp.exp(fresh - top)
    total = jnp.sum(scores, axis=1, keepdims=True) + jnp.sum(fresh, axis=1, keepdims=True)
    lse = top + jnp.log(total)
    inverse = 1.0 / total
    output = jnp.dot(
        (scores * inverse).astype(BF16), cache_ref[0, 0, 1], preferred_element_type=F32
    ) + jnp.dot((fresh * inverse).astype(BF16), new_values, preferred_element_type=F32)
    output = output.astype(BF16)
    out_ref[0] = jnp.concatenate(
        [output[h * steps : (h + 1) * steps] for h in range(heads)], axis=1
    )
    place = lax.broadcasted_iota(jnp.int32, (heads * steps, 128), 0) % steps
    lane = lax.broadcasted_iota(jnp.int32, (heads * steps, 128), 1)
    line = jnp.sum(jnp.where(place == lane, lse, 0.0), axis=0, keepdims=True)
    for c in range(copies):
        lse_ref[c, pl.ds(row, 1), :] = line


def attend(parts, cache, lengths, copies):
    rows, _, _, slots, _ = cache.shape
    count, tall, width = parts.shape
    steps = tall // rows
    heads = width // HD - 2
    return pl.pallas_call(
        functools.partial(attention_kernel, heads, steps, copies),
        grid_spec=pltpu.PrefetchScalarGridSpec(
            num_scalar_prefetch=1,
            grid=(rows,),
            in_specs=[
                pl.BlockSpec((count, tall, width), lambda r, s: (0, 0, 0)),
                pl.BlockSpec((1, 1, 2, slots, HD), lambda r, s: (r, 0, 0, 0, 0)),
            ],
            out_specs=[
                pl.BlockSpec((1, steps, heads * HD), lambda r, s: (r, 0, 0)),
                pl.BlockSpec((copies, 8, 128), lambda r, s: (0, 0, 0)),
            ],
            scratch_shapes=[pltpu.VMEM((rows, steps, width), F32)],
        ),
        out_shape=[
            jax.ShapeDtypeStruct((rows, steps, heads * HD), BF16),
            jax.ShapeDtypeStruct((copies, 8, 128), F32),
        ],
        compiler_params=pltpu.CompilerParams(vmem_limit_bytes=24 << 20),
        cost_estimate=pl.CostEstimate(
            flops=4 * rows * heads * steps * slots * HD,
            bytes_accessed=cache.size * 2,
            transcendentals=rows * heads * steps * slots,
        ),
        name="attend",
    )(lengths, parts, cache)


def ratio_kernel(copies, versions_ref, sums_ref, recorded_ref, ratios_ref, out_ref):
    rows, steps = recorded_ref.shape
    normalizer = jnp.sum(sums_ref[...], axis=0)[:rows, :steps] / H
    ratios = jnp.exp(jnp.clip(normalizer - recorded_ref[...], -2.0, 2.0))
    ratios_ref[...] = ratios
    per_row = jnp.sum(ratios, axis=1, keepdims=True)
    lane = lax.broadcasted_iota(jnp.int32, (1, 128), 1)
    sums = jnp.zeros((1, 128), F32)
    counts = jnp.zeros((1, 128), F32)
    for r in range(rows):
        hit = lane == versions_ref[r]
        sums = sums + jnp.where(hit, per_row[r : r + 1], 0.0)
        counts = counts + jnp.where(hit, float(steps), 0.0)
    line = lax.broadcasted_iota(jnp.int32, (8, 128), 0)
    both = jnp.where(line == 0, sums, jnp.where(line == 1, counts, 0.0))
    for c in range(copies):
        out_ref[c] = both


def ratio_sums(sums, recorded, versions, copies):
    return pl.pallas_call(
        functools.partial(ratio_kernel, copies),
        in_specs=[
            pl.BlockSpec(memory_space=pltpu.SMEM),
            pl.BlockSpec(memory_space=pltpu.VMEM),
            pl.BlockSpec(memory_space=pltpu.VMEM),
        ],
        out_specs=[pl.BlockSpec(memory_space=pltpu.VMEM)] * 2,
        out_shape=[
            jax.ShapeDtypeStruct(recorded.shape, F32),
            jax.ShapeDtypeStruct((copies, 8, 128), F32),
        ],
        name="ratio_sums",
    )(versions, sums, recorded)


def shards(master, moment, second, grad, hidden, cache, lengths, recorded, versions):
    n_tp = lax.axis_size("tp")
    n_fsdp = lax.axis_size("fsdp")
    rows, steps, width = hidden.shape
    tall = rows * steps
    depth = width // n_fsdp
    core = lax.axis_index("fsdp") % 2
    cores = [[i for i in range(n_fsdp) if i % 2 == c] for c in range(2)]
    pairs = [(i, i ^ 1) for i in range(n_fsdp)]
    chips = n_fsdp // 2

    spread = hidden.reshape(tall, n_fsdp, depth).transpose(1, 0, 2)
    spread = lax.all_to_all(spread, "fsdp", 0, 0, tiled=True).reshape(chips, 2, tall, depth)
    to_keep = lax.dynamic_index_in_dim(spread, core, 1, keepdims=False).reshape(-1, depth)
    to_send = lax.dynamic_index_in_dim(spread, 1 - core, 1, keepdims=False).reshape(-1, depth)

    new_master, fresh = adam(master, moment, second, grad, n_tp)
    weights = lax.all_to_all(fresh, "tp", 0, 0, tiled=True).reshape(depth, -1)
    sent = jnp.dot(to_send, weights, preferred_element_type=F32)
    arrived = lax.ppermute(sent, "fsdp", pairs)
    partial = jnp.dot(to_keep, weights, preferred_element_type=F32) + arrived
    parts = lax.all_to_all(
        partial.reshape(chips, tall, -1), "fsdp", 0, 0, tiled=True, axis_index_groups=cores
    )
    attention, lse_sums = attend(parts, cache, lengths, n_tp)
    lse_sums = lax.all_to_all(lse_sums, "tp", 0, 0, tiled=True)
    ratios, version_sums = ratio_sums(lse_sums, recorded, versions, n_fsdp)
    version_sums = jnp.sum(lax.all_to_all(version_sums, "fsdp", 0, 0, tiled=True), axis=0)
    version_means = version_sums[0, :VERSIONS] / jnp.maximum(version_sums[1, :VERSIONS], 1.0)
    return (new_master, attention, ratios, version_means)


def solution(mesh):
    in_specs = (
        P(("fsdp", "tp"), None),
        P(("fsdp", "tp"), None),
        P(("fsdp", "tp"), None),
        P(("fsdp", "tp"), None),
        P("fsdp", None, None),
        P("fsdp", "tp", None, None, None),
        P("fsdp"),
        P("fsdp", None),
        P("fsdp"),
    )
    out_specs = (P(("fsdp", "tp"), None), P("fsdp", None, "tp"), P("fsdp", None), P())
    return jax.shard_map(shards, mesh=mesh, in_specs=in_specs, out_specs=out_specs, check_vma=False)
```

time: 229 us -> 98.5 us (0.43)
  waiting for transfers between devices: 111 us -> 19.4 us
  blocking collectives: 77.8 us -> 38.8 us
  starting transfers between devices: 0.04 us -> 15.5 us
  matrix products: 15.7 us -> 0.69 us
  between operations: 14.1 us -> 0.69 us
  Pallas kernels: 0 us -> 11.5 us
  local copies, waits for them, and re-layouts: 0.86 us -> 10.7 us
  other arithmetic: 9.01 us -> 0.54 us
    all_gather x1 -> x0, waiting for transfers between devices: 111 us -> none  [shards(): lax.all_gather(local_weights, 'fsdp', axis=0, tiled=True)]
    psum x2 -> x0, blocking collectives: 51 us -> none  [the longest x1 30.5 us: shards(): sums, counts = lax.psum((sums, counts), 'fsdp')]
    all_to_all x0 -> x2, waiting for transfers between devices: none -> 17.7 us  [the longest x1 17.7 us: shards(): weights = lax.all_to_all(fresh, 'tp', 0, 0, tiled=True).reshape(depth, -1)]
    dot_general x5 -> x2, matrix products: 15.7 us -> 0.69 us  [the longest x1 0.35 us: shards(): partial = jnp.dot(to_keep, weights, preferred_element_type=F32) + arrived]
    all_to_all x0 -> x2, starting transfers between devices: none -> 14.1 us  [the longest x1 7.22 us: shards(): weights = lax.all_to_all(fresh, 'tp', 0, 0, tiled=True).reshape(depth, -1)]
    all_to_all x1 -> x3, blocking collectives: 26.8 us -> 38.8 us  [the longest x1 14.9 us: shards(): lax.all_to_all(partial.reshape(chips, tall, -1), 'fsdp', 0, 0, tiled=True...]
    pallas_call x0 -> x3, Pallas kernels: none -> 11.5 us  [the longest x1 5.2 us: attend(): pl.pallas_call(functools.partial(attention_kernel, heads, steps, copies),...]
    unnamed x8 -> x12, local copies, waits for them, and re-layouts: 0.03 us -> 8.61 us
  transfers between devices with their start and end apart: 1 -> 3, of which waited for: 1 -> 2; matrix products, arithmetic and copies ran while one was open for 0% -> 0% of each run, Pallas kernels for 0% -> 5%
where the time goes in v1:
time: 98.5 us; the launch traced here: 97.8 us
  blocking collectives  38.8 us (39%)
  waiting for transfers between devices  19.4 us (20%)
  starting transfers between devices  15.5 us (16%)
  Pallas kernels  11.5 us (12%)
  local copies, waits for them, and re-layouts  10.7 us (11%)
    all_to_all x1, waiting for transfers between devices, shards(): weights = lax.all_to_all(fresh, 'tp', 0, 0, tiled=True).reshape(depth, -1)  17.7 us
    all_to_all x1, blocking collectives, shards(): lax.all_to_all(partial.reshape(chips, tall, -1), 'fsdp', 0, 0, tiled=True...  14.9 us
    all_to_all x1, blocking collectives, shards(): lax.all_to_all(version_sums, 'fsdp', 0, 0, tiled=True)  12.5 us
    all_to_all x1, blocking collectives, shards(): lse_sums = lax.all_to_all(lse_sums, 'tp', 0, 0, tiled=True)  11.5 us
    unnamed x12, local copies, waits for them, and re-layouts  8.61 us
    all_to_all x1, starting transfers between devices, shards(): weights = lax.all_to_all(fresh, 'tp', 0, 0, tiled=True).reshape(depth, -1)  7.22 us
    all_to_all x1, starting transfers between devices, shards(): lax.all_to_all(spread, 'fsdp', 0, 0, tiled=True)  6.91 us
    pallas_call x1, Pallas kernels, attend(): pl.pallas_call(functools.partial(attention_kernel, heads, steps, copies),...  5.2 us
  transfers between devices with their start and end apart: 3, of which 2 were waited for; matrix products, arithmetic and copies ran while one was open for 0% of the time, Pallas kernels for 5%

profile of v1, /device:TPU:1, one launch (start us, length us, event | category | flops | bytes accessed | tf_op | source)
XLA Modules:
  0.0 97.8 jit_solution(10003115566602118276)
XLA Ops:
  0.6 0.0 copy-start.4
  0.6 1.2 %reshape.31 = bf16[16,16,512]{2,1,0:T(8,128)(2,1)S(1)} reshape(bf16[4,4,8192]{2,1,0:T(4,128)(2,1)} %param.13) | data formatting | bytes 524288 | tf_op jit(solution)/shard_map/reshape | solution.py:177
  1.9 0.9 copy.14
  2.7 6.9 %all-to-all-start = ((bf16[16,16,512]{2,1,0:T(8,128)(2,1)}), bf16[16,16,512]{2,1,0:T(8,128)(2,1)S(1)}, u32[]{:S(2)}, u32[]{:S(2)}) async-start(bf16[16,16,512]{2,1,0:T(8,128)(2,1)} %copy.14), calls=%async_computation | async-start | bytes 524288 | tf_op jit(solution)/shard_map/all_to_all | solution.py:178
  9.6 0.0 copy-done.4
  9.7 0.0 copy-start.1
  9.7 1.7 %copy-done.1 = f32[64,10240]{1,0:T(8,128)S(1)} copy-done((f32[64,10240]{1,0:T(8,128)S(1)}, f32[64,10240]{1,0:T(8,128)}, u32[]{:S(2)}) %copy-start.1) | copy-done | bytes 2621464
  11.4 0.0 copy-start.2
  11.4 1.7 %copy-done.2 = f32[64,10240]{1,0:T(8,128)S(1)} copy-done((f32[64,10240]{1,0:T(8,128)S(1)}, f32[64,10240]{1,0:T(8,128)}, u32[]{:S(2)}) %copy-start.2) | copy-done | bytes 2621464
  13.1 0.0 copy-start.3
  13.1 1.7 %copy-done.3 = f32[64,10240]{1,0:T(8,128)S(1)} copy-done((f32[64,10240]{1,0:T(8,128)S(1)}, f32[64,10240]{1,0:T(8,128)}, u32[]{:S(2)}) %copy-start.3) | copy-done | bytes 2621464
  14.9 4.8 %adam.1 = (f32[64,10240]{1,0:T(8,128)}, bf16[8,64,1280]{2,1,0:T(8,128)(2,1)}) custom-call(f32[64,10240]{1,0:T(8,128)S(1)} %copy-done.1, f32[64,10240]{1,0:T(8,128)S(1)} %copy-done.2, f32[64,10240]{1,0:T(8,128)S(1)} %copy-done.3, bf16[64,10240]{1,0:T(8,128)(2,1)S(1)} %copy-done.4), custom_call_target="tpu_custom_call" | custom-call | flops 7864320 | bytes 13107200 | tf_op jit(solution)/shard_map/adam/pallas_call | solution.py:31
  19.6 0.0 all-to-all-done
  19.6 7.2 %all-to-all-start.1 = ((bf16[8,64,1280]{2,1,0:T(8,128)(2,1)}), bf16[8,64,1280]{2,1,0:T(8,128)(2,1)S(1)}, u32[]{:S(2)}, u32[]{:S(2)}) async-start(bf16[8,64,1280]{2,1,0:T(8,128)(2,1)} %get-tuple-element.11), calls=%async_computation.1 | async-start | bytes 2621440 | tf_op jit(solution)/shard_map/all_to_all | solution.py:183
  26.9 17.7 %all-to-all-done.1 = bf16[8,64,1280]{2,1,0:T(8,128)(2,1)S(1)} async-done(((bf16[8,64,1280]{2,1,0:T(8,128)(2,1)}), bf16[8,64,1280]{2,1,0:T(8,128)(2,1)S(1)}, u32[]{:S(2)}, u32[]{:S(2)}) %all-to-all-start.1) | async-done | bytes 1310752 | tf_op jit(solution)/shard_map/all_to_all | solution.py:183
  44.6 0.3 fusion.1
  44.9 1.3 %collective-permute-start = (f32[128,1280]{1,0:T(8,128)S(1)}, f32[128,1280]{1,0:T(8,128)S(1)}, u32[]{:S(2)}, u32[]{:S(2)}) collective-permute-start(f32[128,1280]{1,0:T(8,128)S(1)} %fusion.1), channel_id=1, source_target_pairs={{0,8},{8,0},{16,24},{24,16},{32,40},{40,32},{48,56},{56,48},{64,72... | collective-permute-start | bytes 1966088 | tf_op jit(solution)/shard_map/ppermute | solution.py:185
  46.2 1.7 %collective-permute-done = f32[128,1280]{1,0:T(8,128)S(1)} collective-permute-done((f32[128,1280]{1,0:T(8,128)S(1)}, f32[128,1280]{1,0:T(8,128)S(1)}, u32[]{:S(2)}, u32[]{:S(2)}) %collective-permute-start) | collective-permute-done | bytes 655392 | tf_op jit(solution)/shard_map/ppermute | solution.py:185
  48.0 0.4 convolution_add_fusion
  48.3 0.0 copy-start.5
  48.3 14.9 %all_to_all.25.parts_ref = f32[8,16,1280]{2,1,0:T(8,128)S(1)} all-to-all(f32[8,16,1280]{2,1,0:T(8,128)S(1)} %bitcast.14), channel_id=1, replica_groups={{0,16,32,48,64,80,96,112},{8,24,40,56,72,88,104,120},{1,17,33,49,65,81,..., dimensions={0} | all-to-all | bytes 1310720 | tf_op jit(solution)/shard_map/all_to_all | solution.py:187
  63.2 0.0 copy-done.5
  63.2 0.0 copy-start
  63.2 3.4 %copy-done = bf16[4,1,2,4096,128]{4,3,2,1,0:T(8,128)(2,1)S(1)} copy-done((bf16[4,1,2,4096,128]{4,3,2,1,0:T(8,128)(2,1)S(1)}, bf16[4,1,2,4096,128]{4,3,2,1,0:T(8,128)(2,1)}, u32[]{:S(2)}) %copy-start) | copy-done | bytes 8388632
  66.6 5.2 %attend.1 = (bf16[4,4,1024]{2,1,0:T(4,128)(2,1)}, f32[8,8,128]{2,1,0:T(8,128)S(1)}) custom-call(s32[4]{0:T(128)S(1)} %copy-done.5, f32[8,16,1280]{2,1,0:T(8,128)S(1)} %all_to_all.25.parts_ref, bf16[4,1,2,4096,128]{4,3,2,1,0:T(8,128)(2,1)S(1)} %copy-done), custom_call_target="tpu_custom_call" | custom-call | flops 268435456 | bytes 8388608 | tf_op jit(solution)/shard_map/attend/pallas_call | solution.py:101
  71.8 11.5 %all_to_all.26.sums_ref = f32[8,8,128]{2,1,0:T(8,128)} all-to-all(f32[8,8,128]{2,1,0:T(8,128)S(1)} %get-tuple-element.13), channel_id=1, replica_groups=mesh['fsdp'=16,'tp'=8] {'tp'}, dimensions={0} | all-to-all | bytes 65536 | tf_op jit(solution)/shard_map/all_to_all | solution.py:191
  83.3 1.5 %ratio_sums.1 = (f32[4,4]{1,0:T(4,128)}, f32[16,8,128]{2,1,0:T(8,128)}) custom-call(s32[4]{0:T(128)} %versions_ref.1, f32[8,8,128]{2,1,0:T(8,128)} %all_to_all.26.sums_ref, f32[4,4]{1,0:T(4,128)} %recorded_ref.1), custom_call_target="tpu_custom_call" | custom-call | tf_op jit(solution)/shard_map/ratio_sums/pallas_call | solution.py:150
  84.8 12.5 %all_to_all.27 = f32[16,8,128]{2,1,0:T(8,128)S(1)} all-to-all(f32[16,8,128]{2,1,0:T(8,128)} %get-tuple-element.15), channel_id=1, replica_groups=mesh['fsdp'=16,'tp'=8] {'fsdp'}, dimensions={0} | all-to-all | bytes 131072 | tf_op jit(solution)/shard_map/all_to_all | solution.py:193
  97.3 0.5 fusion
  (2 shorter events, 0.0 us)
Async XLA Ops:
  0.6 9.0 %copy-start.4 = (bf16[64,10240]{1,0:T(8,128)(2,1)S(1)}, bf16[64,10240]{1,0:T(8,128)(2,1)}, u32[]{:S(2)}) copy-start(bf16[64,10240]{1,0:T(8,128)(2,1)} %grad_ref.1) | copy-start | bytes 3932164
  2.7 16.9 %all-to-all-start = ((bf16[16,16,512]{2,1,0:T(8,128)(2,1)}), bf16[16,16,512]{2,1,0:T(8,128)(2,1)S(1)}, u32[]{:S(2)}, u32[]{:S(2)}) async-start(bf16[16,16,512]{2,1,0:T(8,128)(2,1)} %copy.14), calls=%async_computation | async-start | bytes 524288 | tf_op jit(solution)/shard_map/all_to_all | solution.py:178
  9.7 1.7 %copy-start.1 = (f32[64,10240]{1,0:T(8,128)S(1)}, f32[64,10240]{1,0:T(8,128)}, u32[]{:S(2)}) copy-start(f32[64,10240]{1,0:T(8,128)} %master_ref.1) | copy-start | bytes 7864324
  11.4 1.7 %copy-start.2 = (f32[64,10240]{1,0:T(8,128)S(1)}, f32[64,10240]{1,0:T(8,128)}, u32[]{:S(2)}) copy-start(f32[64,10240]{1,0:T(8,128)} %moment_ref.1) | copy-start | bytes 7864324
  13.1 1.7 %copy-start.3 = (f32[64,10240]{1,0:T(8,128)S(1)}, f32[64,10240]{1,0:T(8,128)}, u32[]{:S(2)}) copy-start(f32[64,10240]{1,0:T(8,128)} %second_ref.1) | copy-start | bytes 7864324
  19.6 24.9 %all-to-all-start.1 = ((bf16[8,64,1280]{2,1,0:T(8,128)(2,1)}), bf16[8,64,1280]{2,1,0:T(8,128)(2,1)S(1)}, u32[]{:S(2)}, u32[]{:S(2)}) async-start(bf16[8,64,1280]{2,1,0:T(8,128)(2,1)} %get-tuple-element.11), calls=%async_computation.1 | async-start | bytes 2621440 | tf_op jit(solution)/shard_map/all_to_all | solution.py:183
  44.9 3.0 %collective-permute-start = (f32[128,1280]{1,0:T(8,128)S(1)}, f32[128,1280]{1,0:T(8,128)S(1)}, u32[]{:S(2)}, u32[]{:S(2)}) collective-permute-start(f32[128,1280]{1,0:T(8,128)S(1)} %fusion.1), channel_id=1, source_target_pairs={{0,8},{8,0},{16,24},{24,16},{32,40},{40,32},{48,56},{56,48},{64,72... | collective-permute-start | bytes 1966088 | tf_op jit(solution)/shard_map/ppermute | solution.py:185
  48.3 14.9 %copy-start.5 = (s32[4]{0:T(128)S(1)}, s32[4]{0:T(128)}, u32[]{:S(2)}) copy-start(s32[4]{0:T(128)} %lengths_ref.1) | copy-start | bytes 52
  63.2 3.4 %copy-start = (bf16[4,1,2,4096,128]{4,3,2,1,0:T(8,128)(2,1)S(1)}, bf16[4,1,2,4096,128]{4,3,2,1,0:T(8,128)(2,1)}, u32[]{:S(2)}) copy-start(bf16[4,1,2,4096,128]{4,3,2,1,0:T(8,128)(2,1)} %cache_ref.1) | copy-start | bytes 25165828

commit v2 on v0

v2 whole, which is shorter than its diff:
```python
import functools

import jax
import jax.numpy as jnp
from jax import lax
from jax.experimental import pallas as pl
from jax.experimental.pallas import tpu as pltpu
from jax.sharding import PartitionSpec as P

H = 64
HD = 128
VERSIONS = 4
F32 = jnp.float32
BF16 = jnp.bfloat16
ANY = pl.BlockSpec(memory_space=pl.ANY)
VMEM = pl.BlockSpec(memory_space=pltpu.VMEM)
SMEM = pl.BlockSpec(memory_space=pltpu.SMEM)
MIB = 1 << 20
in_hbm = functools.partial(pltpu.with_memory_space_constraint, memory_space=pltpu.HBM)
in_vmem = functools.partial(pltpu.with_memory_space_constraint, memory_space=pltpu.VMEM)
LOG2E = 1.4426950408889634
AHEAD = 3
HOPS = (8, 1, 2, 6)


def adam_kernel(master, moment, second, grad, new, weights, a, b, c, g, n, w, arrive, leave):
    parts, rows, width = w.shape
    sources = ((master, a), (moment, b), (second, c), (grad, g))

    def columns(i):
        return pl.ds(i * width, width)

    def fetches(i):
        return [
            pltpu.make_async_copy(hbm.at[:, columns(i)], buf.at[i], arrive.at[i, k])
            for k, (hbm, buf) in enumerate(sources)
        ]

    def stores(i):
        return [
            pltpu.make_async_copy(n.at[i], new.at[:, columns(i)], leave.at[i, 0]),
            pltpu.make_async_copy(w.at[i], weights.at[i], leave.at[i, 1]),
        ]

    for i in range(AHEAD):
        for copy in fetches(i):
            copy.start()
    for i in range(parts):
        if i + AHEAD < parts:
            for copy in fetches(i + AHEAD):
                copy.start()
        for copy in fetches(i):
            copy.wait()

        def tile(k, carry, i=i):
            at = pl.ds(pl.multiple_of(k * 16, 16), 16)
            gradient = g[i, at].astype(F32)
            fresh_moment = 0.9 * b[i, at] + 0.1 * gradient
            fresh_second = 0.95 * c[i, at] + 0.05 * gradient * gradient
            spread = jnp.sqrt(fresh_second * (1.0 / (1.0 - 0.95**10))) + 1e-08
            fresh = a[i, at] - (0.005 / (1.0 - 0.9**10)) * fresh_moment / spread
            n[i, at] = fresh
            w[i, at] = fresh.astype(BF16)
            return carry

        lax.fori_loop(0, rows // 16, tile, 0)
        for copy in stores(i):
            copy.start()
    for i in range(parts):
        for copy in stores(i):
            copy.wait()


def adam(master, moment, second, grad, parts):
    rows, columns = master.shape
    width = columns // parts
    return pl.pallas_call(
        adam_kernel,
        in_specs=[ANY] * 4,
        out_specs=[ANY] * 2,
        out_shape=[
            jax.ShapeDtypeStruct((rows, columns), F32),
            jax.ShapeDtypeStruct((parts, rows, width), BF16),
        ],
        scratch_shapes=[
            pltpu.VMEM((parts, rows, width), F32),
            pltpu.VMEM((parts, rows, width), F32),
            pltpu.VMEM((parts, rows, width), F32),
            pltpu.VMEM((parts, rows, width), BF16),
            pltpu.VMEM((parts, rows, width), F32),
            pltpu.VMEM((parts, rows, width), BF16),
            pltpu.SemaphoreType.DMA((parts, 4)),
            pltpu.SemaphoreType.DMA((parts, 2)),
        ],
        compiler_params=pltpu.CompilerParams(vmem_limit_bytes=60 * MIB),
        cost_estimate=pl.CostEstimate(
            flops=12 * rows * columns, bytes_accessed=20 * rows * columns, transcendentals=0
        ),
        name="adam",
    )(master, moment, second, grad)


def offset(i):
    total = 0
    for k, hop in enumerate(HOPS):
        if i >> (len(HOPS) - 1 - k) & 1:
            total ^= hop
    return total


def stage_kernel(lengths, versions, recorded, hidden, meta, spread):
    rows, steps = recorded.shape
    lane = lax.broadcasted_iota(jnp.int32, (1, 128), 1)
    line = jnp.zeros((1, 128), F32)
    for r in range(rows):
        for s in range(steps):
            at = r * steps + s
            line = jnp.where(lane == rows * steps + at, recorded[r, s], line)
            line = jnp.where(lane == 2 * rows * steps + at, versions[r].astype(F32), line)
    meta[0:1] = line
    for r in range(rows):
        meta[r + 1 : r + 2] = jnp.full((1, 128), lengths[r].astype(F32))
    me = lax.axis_index("fsdp")
    depth = spread.shape[2]
    for f in range(spread.shape[0]):
        at = pl.ds(pl.multiple_of((me ^ offset(f)) * depth, depth), depth)
        for r in range(rows):
            spread[f, r * steps : (r + 1) * steps] = hidden[r, :, at]


def stage(lengths, versions, recorded, hidden, n_fsdp):
    rows, steps, width = hidden.shape
    return pl.pallas_call(
        stage_kernel,
        in_specs=[SMEM, SMEM, SMEM, VMEM],
        out_specs=[VMEM] * 2,
        out_shape=[
            jax.ShapeDtypeStruct((8, 128), F32),
            jax.ShapeDtypeStruct((n_fsdp, rows * steps, width // n_fsdp), BF16),
        ],
        compiler_params=pltpu.CompilerParams(vmem_limit_bytes=16 * MIB),
        name="stage",
    )(in_hbm(lengths), in_hbm(versions), in_hbm(recorded), in_hbm(hidden))


def product_kernel(flip, spread, weights, out):
    me = lax.axis_index("fsdp")
    chips = out.shape[0] // spread.shape[1]
    where = {offset(i): i for i in range(spread.shape[0])}
    blocks = []
    for chip in range(chips):
        away = me ^ flip ^ (2 * chip + (me & 1))
        at = jnp.int32(0)
        for far, i in where.items():
            at = jnp.where(away == far, i, at)
        blocks.append(spread[at])
    out[...] = jnp.dot(
        jnp.concatenate(blocks, axis=0), weights[...], preferred_element_type=F32
    )


def product(spread, weights, n_fsdp, flip):
    _, tall, depth = spread.shape
    width = weights.shape[1]
    return pl.pallas_call(
        functools.partial(product_kernel, flip),
        in_specs=[VMEM] * 2,
        out_specs=VMEM,
        out_shape=jax.ShapeDtypeStruct((n_fsdp // 2 * tall, width), F32),
        compiler_params=pltpu.CompilerParams(vmem_limit_bytes=16 * MIB),
        cost_estimate=pl.CostEstimate(
            flops=n_fsdp * tall * depth * width, bytes_accessed=16 * MIB, transcendentals=0
        ),
        name="product",
    )(spread, weights)


def score_kernel(steps, parts, cache, meta, probs, base, lse_out):
    rows = cache.shape[0]
    heads = parts.shape[2] // HD - 2
    total = parts[0]
    for i in range(1, parts.shape[0]):
        total = total + parts[i]
    scale = HD ** (-0.5)
    contract = (((1,), (1,)), ((), ()))
    line = meta[0:1]
    for r in range(rows):
        mine = total[r * steps : (r + 1) * steps]
        queries = jnp.concatenate(
            [mine[:, h * HD : (h + 1) * HD] for h in range(heads)], axis=0
        ).astype(BF16)
        new_keys = mine[:, heads * HD : (heads + 1) * HD].astype(BF16)
        new_values = mine[:, (heads + 1) * HD :].astype(BF16)
        old = lax.dot_general(queries, cache[r, 0, 0], contract, preferred_element_type=F32)
        slot = lax.broadcasted_iota(jnp.int32, old.shape, 1).astype(F32)
        old = jnp.where(slot < meta[r + 1 : r + 2, 0:1], old, -1e31)
        new = lax.dot_general(queries, new_keys, contract, preferred_element_type=F32)
        step = lax.broadcasted_iota(jnp.int32, new.shape, 0) % steps
        later = lax.broadcasted_iota(jnp.int32, new.shape, 1)
        new = jnp.where(later <= step, new, -1e31)
        top = jnp.maximum(
            jnp.max(old, axis=1, keepdims=True), jnp.max(new, axis=1, keepdims=True)
        )
        old = jnp.exp2((old - top) * (scale * LOG2E))
        new = jnp.exp2((new - top) * (scale * LOG2E))
        mass = jnp.sum(old, axis=1, keepdims=True) + jnp.sum(new, axis=1, keepdims=True)
        lse = top * scale + jnp.log(mass)
        inverse = 1.0 / mass
        probs[r] = (old * inverse).astype(BF16)
        base[r] = jnp.dot((new * inverse).astype(BF16), new_values, preferred_element_type=F32)
        place = lax.broadcasted_iota(jnp.int32, (heads * steps, 128), 0) % steps + r * steps
        lane = lax.broadcasted_iota(jnp.int32, (heads * steps, 128), 1)
        line = line + jnp.sum(jnp.where(place == lane, lse, 0.0), axis=0, keepdims=True)
    lse_out[...] = jnp.broadcast_to(line, lse_out.shape)


def score(parts, cache, meta, steps, copies):
    rows, _, _, slots, _ = cache.shape
    heads = parts.shape[2] // HD - 2
    return pl.pallas_call(
        functools.partial(score_kernel, steps),
        in_specs=[VMEM] * 3,
        out_specs=[VMEM] * 3,
        out_shape=[
            jax.ShapeDtypeStruct((rows, heads * steps, slots), BF16),
            jax.ShapeDtypeStruct((rows, heads * steps, HD), F32),
            jax.ShapeDtypeStruct((copies, 128), F32),
        ],
        compiler_params=pltpu.CompilerParams(vmem_limit_bytes=24 * MIB),
        cost_estimate=pl.CostEstimate(
            flops=2 * rows * heads * steps * slots * HD,
            bytes_accessed=cache.size,
            transcendentals=rows * heads * steps * slots,
        ),
        name="score",
    )(parts, in_vmem(cache), meta)


def mix_kernel(steps, probs, base, values, out):
    tall = probs.shape[1]
    mixed = jnp.dot(probs[0], values[0, 0, 0], preferred_element_type=F32) + base[0]
    mixed = mixed.astype(BF16)
    out[0] = jnp.concatenate(
        [mixed[h * steps : (h + 1) * steps] for h in range(tall // steps)], axis=1
    )


def mix(probs, base, cache, steps):
    rows, tall, slots = probs.shape
    width = tall // steps * HD
    return pl.pallas_call(
        functools.partial(mix_kernel, steps),
        grid=(rows,),
        in_specs=[
            pl.BlockSpec((1, tall, slots), lambda r: (r, 0, 0)),
            pl.BlockSpec((1, tall, HD), lambda r: (r, 0, 0)),
            pl.BlockSpec((1, 1, 1, slots, HD), lambda r: (r, 0, 1, 0, 0)),
        ],
        out_specs=pl.BlockSpec((1, steps, width), lambda r: (r, 0, 0)),
        out_shape=jax.ShapeDtypeStruct((rows, steps, width), BF16),
        compiler_params=pltpu.CompilerParams(vmem_limit_bytes=24 * MIB),
        cost_estimate=pl.CostEstimate(
            flops=2 * rows * tall * slots * HD, bytes_accessed=cache.size, transcendentals=0
        ),
        name="mix",
    )(probs, base, in_hbm(cache))


def ratio_kernel(gathered, ratios, means):
    rows, steps = ratios.shape
    count = rows * steps
    n_fsdp = lax.axis_size("fsdp")
    n_tp = gathered.shape[0] // n_fsdp
    lines = gathered[...].reshape(n_fsdp, n_tp, 128)
    normalizer = jnp.sum(lines, axis=1)[:, :count] / H
    first = lines[:, 0]
    recorded = first[:, count : 2 * count]
    version = first[:, 2 * count : 3 * count]
    ratio = jnp.exp(jnp.clip(normalizer - recorded, -2.0, 2.0))
    for v in range(VERSIONS):
        hit = version == float(v)
        members = jnp.sum(jnp.where(hit, 1.0, 0.0))
        means[v] = jnp.sum(jnp.where(hit, ratio, 0.0)) / jnp.maximum(members, 1.0)
    group = lax.broadcasted_iota(jnp.int32, ratio.shape, 0)
    mine = jnp.sum(
        jnp.where(group == lax.axis_index("fsdp"), ratio, 0.0), axis=0, keepdims=True
    )
    for r in range(rows):
        ratios[r : r + 1] = mine[:, r * steps : (r + 1) * steps]


def final(gathered, rows, steps):
    return pl.pallas_call(
        ratio_kernel,
        in_specs=[VMEM],
        out_specs=[VMEM, SMEM],
        out_shape=[
            jax.ShapeDtypeStruct((rows, steps), F32),
            jax.ShapeDtypeStruct((VERSIONS,), F32),
        ],
        name="ratios",
    )(in_vmem(gathered))


def shards(master, moment, second, grad, hidden, cache, lengths, recorded, versions):
    n_tp = lax.axis_size("tp")
    n_fsdp = lax.axis_size("fsdp")
    rows, steps, width = hidden.shape
    tall = rows * steps
    depth = width // n_fsdp
    chips = n_fsdp // 2
    cores = [[i for i in range(n_fsdp) if i % 2 == c] for c in range(2)]
    pairs = [(i, i ^ 1) for i in range(n_fsdp)]

    meta, spread = stage(lengths, versions, recorded, hidden, n_fsdp)
    new_master, fresh = adam(master, moment, second, grad, n_tp)
    for k, hop in enumerate(HOPS):
        halves = spread.reshape(2**k, 2, -1, tall, depth)
        moved = lax.ppermute(halves[:, 1], "fsdp", [(i, i ^ hop) for i in range(n_fsdp)])
        if k == 0:
            moved, fresh = lax.optimization_barrier((moved, fresh))
        spread = jnp.stack([halves[:, 0], moved], axis=1)
    spread = spread.reshape(n_fsdp, tall, depth)
    weights = lax.all_to_all(fresh, "tp", 0, 0, tiled=True).reshape(depth, -1)

    sent = product(spread, weights, n_fsdp, 1)
    arrived = lax.ppermute(sent, "fsdp", pairs)
    partial = product(spread, weights, n_fsdp, 0) + arrived
    parts = lax.all_to_all(
        partial.reshape(chips, tall, -1), "fsdp", 0, 0, tiled=True, axis_index_groups=cores
    )
    probs, base, lines = score(parts, cache, meta, steps, n_fsdp * n_tp)
    lines = lax.all_to_all(lines, ("fsdp", "tp"), 0, 0, tiled=True)
    attention = mix(probs, base, cache, steps)
    ratios, version_means = final(lines, rows, steps)
    return (new_master, attention, ratios, version_means)


def solution(mesh):
    in_specs = (
        P(("fsdp", "tp"), None),
        P(("fsdp", "tp"), None),
        P(("fsdp", "tp"), None),
        P(("fsdp", "tp"), None),
        P("fsdp", None, None),
        P("fsdp", "tp", None, None, None),
        P("fsdp"),
        P("fsdp", None),
        P("fsdp"),
    )
    out_specs = (P(("fsdp", "tp"), None), P("fsdp", None, "tp"), P("fsdp", None), P())
    return jax.shard_map(shards, mesh=mesh, in_specs=in_specs, out_specs=out_specs, check_vma=False)
```

time: 229 us -> 78.5 us (0.34)
  waiting for transfers between devices: 111 us -> 19.7 us
  blocking collectives: 77.8 us -> 14.6 us
  starting transfers between devices: 0.04 us -> 22.8 us
  Pallas kernels: 0 us -> 16.6 us
  matrix products: 15.7 us -> 0 us
  between operations: 14.1 us -> 0.74 us
  other arithmetic: 9.01 us -> 0.17 us
  local copies, waits for them, and re-layouts: 0.86 us -> 3.46 us
    all_gather x1 -> x0, waiting for transfers between devices: 111 us -> none  [shards(): lax.all_gather(local_weights, 'fsdp', axis=0, tiled=True)]
    psum x2 -> x0, blocking collectives: 51 us -> none  [the longest x1 30.5 us: shards(): sums, counts = lax.psum((sums, counts), 'fsdp')]
    pallas_call x0 -> x7, Pallas kernels: none -> 16.6 us  [the longest x1 6.11 us: adam(): pl.pallas_call(adam_kernel, in_specs=[ANY] * 4, out_specs=[ANY] * 2, out_...]
    dot_general x5 -> x0, matrix products: 15.7 us -> none  [the longest x1 8.43 us: shards(): jnp.dot(flat_rows, lax.all_gather(local_weights, 'fsdp', axis=0, tiled=Tr...]
    all_to_all x0 -> x2, starting transfers between devices: none -> 14.2 us  [the longest x1 7.2 us: shards(): weights = lax.all_to_all(fresh, 'tp', 0, 0, tiled=True).reshape(depth, -1)]
    all_to_all x0 -> x2, waiting for transfers between devices: none -> 12.3 us  [the longest x1 7.24 us: shards(): weights = lax.all_to_all(fresh, 'tp', 0, 0, tiled=True).reshape(depth, -1)]
    all_to_all x1, blocking collectives: 26.8 us -> 14.6 us  [shards(): lax.all_to_all(partial.reshape(chips, tall, -1), 'fsdp', 0, 0, tiled=True...]
    ppermute x0 -> x5, starting transfers between devices: none -> 8.61 us  [the longest x4 7.34 us: shards(): lax.ppermute(halves[:, 1], 'fsdp', [(i, i ^ hop) for i in range(n_fsdp)])]
  transfers between devices with their start and end apart: 1 -> 7, of which waited for: 1 -> 5; matrix products, arithmetic and copies ran while one was open for 0% -> 0% of each run, Pallas kernels for 0% -> 14%
where the time goes in v2:
time: 78.5 us; the launch traced here: 78.1 us
  starting transfers between devices  22.8 us (29%)
  waiting for transfers between devices  19.7 us (25%)
  Pallas kernels  16.6 us (21%)
  blocking collectives  14.6 us (19%)
  local copies, waits for them, and re-layouts  3.46 us (4%)
    all_to_all x1, blocking collectives, shards(): lax.all_to_all(partial.reshape(chips, tall, -1), 'fsdp', 0, 0, tiled=True...  14.6 us
    ppermute x4, starting transfers between devices, shards(): lax.ppermute(halves[:, 1], 'fsdp', [(i, i ^ hop) for i in range(n_fsdp)])  7.34 us
    all_to_all x1, waiting for transfers between devices, shards(): weights = lax.all_to_all(fresh, 'tp', 0, 0, tiled=True).reshape(depth, -1)  7.24 us
    all_to_all x1, starting transfers between devices, shards(): weights = lax.all_to_all(fresh, 'tp', 0, 0, tiled=True).reshape(depth, -1)  7.2 us
    all_to_all x1, starting transfers between devices, shards(): lines = lax.all_to_all(lines, ('fsdp', 'tp'), 0, 0, tiled=True)  7.03 us
    ppermute x4, waiting for transfers between devices, shards(): lax.ppermute(halves[:, 1], 'fsdp', [(i, i ^ hop) for i in range(n_fsdp)])  6.14 us
    pallas_call x1, Pallas kernels, adam(): pl.pallas_call(adam_kernel, in_specs=[ANY] * 4, out_specs=[ANY] * 2, out_...  6.11 us
    all_to_all x1, waiting for transfers between devices, shards(): lines = lax.all_to_all(lines, ('fsdp', 'tp'), 0, 0, tiled=True)  5.02 us
  transfers between devices with their start and end apart: 7, of which 5 were waited for; matrix products, arithmetic and copies ran while one was open for 0% of the time, Pallas kernels for 14%

profile of v2, /device:TPU:1, one launch (start us, length us, event | category | flops | bytes accessed | tf_op | source)
XLA Modules:
  0.0 78.1 jit_solution(10628020985200635805)
XLA Ops:
  0.6 1.0 %stage.1 = (f32[8,128]{1,0:T(8,128)S(1)}, bf16[16,16,512]{2,1,0:T(8,128)(2,1)S(1)}) custom-call(s32[4]{0:T(128)} %lengths.1, s32[4]{0:T(128)} %versions.1, f32[4,4]{1,0:T(4,128)} %recorded.1, bf16[4,4,8192]{2,1,0:T(4,128)(2,1)} %hidden.1), custom_call_target="tpu_custom_call" | custom-call | tf_op jit(solution)/shard_map/stage/pallas_call | solution.py:133
  1.7 2.1 %collective-permute-start = (bf16[1,8,16,512]{3,2,1,0:T(8,128)(2,1)S(1)}, bf16[1,8,16,512]{3,2,1,0:T(8,128)(2,1)S(1)}, u32[]{:S(2)}, u32[]{:S(2)}) collective-permute-start(bf16[1,8,16,512]{3,2,1,0:T(8,128)(2,1)S(1)} %get-tuple-element.33), channel_id=1, source_target_pairs={{0,64},{8,72},{16,80},{24,88},{32,96},{40,104},{48,112},{56,120},{... | collective-permute-start | bytes 393224 | tf_op jit(solution)/shard_map/ppermute | solution.py:319
  3.8 6.1 %adam.1 = (f32[64,10240]{1,0:T(8,128)}, bf16[8,64,1280]{2,1,0:T(8,128)(2,1)}) custom-call(f32[64,10240]{1,0:T(8,128)} %master.1, f32[64,10240]{1,0:T(8,128)} %moment.1, f32[64,10240]{1,0:T(8,128)} %second.1, bf16[64,10240]{1,0:T(8,128)(2,1)} %grad.1), custom_call_target="tpu_custom_call" | custom-call | flops 7864320 | bytes 13107200 | tf_op jit(solution)/shard_map/adam/pallas_call | solution.py:77
  10.0 0.0 collective-permute-done
  10.0 1.0 %collective-permute-start.1 = (bf16[2,4,16,512]{3,2,1,0:T(8,128)(2,1)S(1)}, bf16[2,4,16,512]{3,2,1,0:T(8,128)(2,1)S(1)}, u32[]{:S(2)}, u32[]{:S(2)}) collective-permute-start(bf16[2,4,16,512]{3,2,1,0:T(8,128)(2,1)S(1)} %get-tuple-element.31), channel_id=1, source_target_pairs={{0,8},{8,0},{16,24},{24,16},{32,40},{40,32},{48,56},{56,48},{64,72... | collective-permute-start | bytes 393224 | tf_op jit(solution)/shard_map/ppermute | solution.py:319
  11.0 7.2 %all-to-all-start = ((bf16[8,64,1280]{2,1,0:T(8,128)(2,1)}), bf16[8,64,1280]{2,1,0:T(8,128)(2,1)S(1)}, u32[]{:S(2)}, u32[]{:S(2)}) async-start(bf16[8,64,1280]{2,1,0:T(8,128)(2,1)} %get-tuple-element.19), calls=%async_computation | async-start | bytes 2621440 | tf_op jit(solution)/shard_map/all_to_all | solution.py:324
  18.2 0.0 collective-permute-done.1
  18.3 1.4 %collective-permute-start.2 = (bf16[4,2,16,512]{3,2,0,1:T(8,128)(2,1)S(1)}, bf16[4,2,16,512]{3,2,0,1:T(8,128)(2,1)S(1)}, u32[]{:S(2)}, u32[]{:S(2)}) collective-permute-start(bf16[4,2,16,512]{3,2,0,1:T(8,128)(2,1)S(1)} %get-tuple-element.29), channel_id=1, source_target_pairs={{0,16},{8,24},{16,0},{24,8},{32,48},{40,56},{48,32},{56,40},{64,80... | collective-permute-start | bytes 393224 | tf_op jit(solution)/shard_map/ppermute | solution.py:319
  19.7 3.5 %collective-permute-done.2 = bf16[4,2,16,512]{3,2,0,1:T(8,128)(2,1)S(1)} collective-permute-done((bf16[4,2,16,512]{3,2,0,1:T(8,128)(2,1)S(1)}, bf16[4,2,16,512]{3,2,0,1:T(8,128)(2,1)S(1)}, u32[]{:S(2)}, u32[]{:S(2)}) %collective-permute-start.2) | collective-permute-done | bytes 131104 | tf_op jit(solution)/shard_map/ppermute | solution.py:319
  23.2 2.8 %collective-permute-start.3 = (bf16[8,1,16,512]{3,2,0,1:T(8,128)(2,1)S(1)}, bf16[8,1,16,512]{3,2,0,1:T(8,128)(2,1)S(1)}, u32[]{:S(2)}, u32[]{:S(2)}) collective-permute-start(bf16[8,1,16,512]{3,2,0,1:T(8,128)(2,1)S(1)} %get-tuple-element.27), channel_id=1, source_target_pairs={{0,48},{8,56},{16,32},{24,40},{32,16},{40,24},{48,0},{56,8},{64,11... | collective-permute-start | bytes 393224 | tf_op jit(solution)/shard_map/ppermute | solution.py:319
  26.1 2.7 %collective-permute-done.3 = bf16[8,1,16,512]{3,2,0,1:T(8,128)(2,1)S(1)} collective-permute-done((bf16[8,1,16,512]{3,2,0,1:T(8,128)(2,1)S(1)}, bf16[8,1,16,512]{3,2,0,1:T(8,128)(2,1)S(1)}, u32[]{:S(2)}, u32[]{:S(2)}) %collective-permute-start.3) | collective-permute-done | bytes 131104 | tf_op jit(solution)/shard_map/ppermute | solution.py:319
  28.7 7.2 %all-to-all-done = bf16[8,64,1280]{2,1,0:T(8,128)(2,1)S(1)} async-done(((bf16[8,64,1280]{2,1,0:T(8,128)(2,1)}), bf16[8,64,1280]{2,1,0:T(8,128)(2,1)S(1)}, u32[]{:S(2)}, u32[]{:S(2)}) %all-to-all-start) | async-done | bytes 1310752 | tf_op jit(solution)/shard_map/all_to_all | solution.py:324
  36.0 0.4 product.3
  36.4 1.3 %collective-permute-start.4 = (f32[128,1280]{1,0:T(8,128)S(1)}, f32[128,1280]{1,0:T(8,128)S(1)}, u32[]{:S(2)}, u32[]{:S(2)}) collective-permute-start(f32[128,1280]{1,0:T(8,128)S(1)} %product.3), channel_id=1, source_target_pairs={{0,8},{8,0},{16,24},{24,16},{32,40},{40,32},{48,56},{56,48},{64,72... | collective-permute-start | bytes 1966088 | tf_op jit(solution)/shard_map/ppermute | solution.py:327
  37.6 0.4 product.2
  38.0 1.3 %collective-permute-done.4 = f32[128,1280]{1,0:T(8,128)S(1)} collective-permute-done((f32[128,1280]{1,0:T(8,128)S(1)}, f32[128,1280]{1,0:T(8,128)S(1)}, u32[]{:S(2)}, u32[]{:S(2)}) %collective-permute-start.4) | collective-permute-done | bytes 655392 | tf_op jit(solution)/shard_map/ppermute | solution.py:327
  39.4 0.1 add.3
  39.4 14.6 %all_to_all.21.parts = f32[8,16,1280]{2,1,0:T(8,128)S(1)} all-to-all(f32[8,16,1280]{2,1,0:T(8,128)S(1)} %bitcast.35), channel_id=1, replica_groups={{0,16,32,48,64,80,96,112},{8,24,40,56,72,88,104,120},{1,17,33,49,65,81,..., dimensions={0} | all-to-all | bytes 1310720 | tf_op jit(solution)/shard_map/all_to_all | solution.py:329
  54.0 0.0 copy-start
  54.0 3.4 %copy-done = bf16[4,1,2,4096,128]{4,3,2,1,0:T(8,128)(2,1)S(1)} copy-done((bf16[4,1,2,4096,128]{4,3,2,1,0:T(8,128)(2,1)S(1)}, bf16[4,1,2,4096,128]{4,3,2,1,0:T(8,128)(2,1)}, u32[]{:S(2)}) %copy-start) | copy-done | bytes 8388632
  57.4 3.3 %score.1 = (bf16[4,32,4096]{2,1,0:T(8,128)(2,1)S(1)}, f32[4,32,128]{2,1,0:T(8,128)S(1)}, f32[128,128]{1,0:T(8,128)}) custom-call(f32[8,16,1280]{2,1,0:T(8,128)S(1)} %all_to_all.21.parts, bf16[4,1,2,4096,128]{4,3,2,1,0:T(8,128)(2,1)S(1)} %copy-done, f32[8,128]{1,0:T(8,128)S(1)} %get-tuple-element.20.meta), custom_call_target="tpu_custom_call" | custom-call | flops 134217728 | bytes 4194304 | tf_op jit(solution)/shard_map/score/pallas_call | solution.py:220
  60.7 7.0 %all-to-all-start.2 = ((f32[128,1,128]{2,1,0:T(1,128)}), f32[128,1,128]{2,1,0:T(1,128)S(1)}, u32[]{:S(2)}, u32[]{:S(2)}) async-start(f32[128,1,128]{2,1,0:T(1,128)} %bitcast.18), calls=%async_computation.2 | async-start | bytes 131072 | tf_op jit(solution)/shard_map/all_to_all | solution.py:333
  67.7 4.3 %mix.1 = bf16[4,4,1024]{2,1,0:T(4,128)(2,1)} custom-call(bf16[4,32,4096]{2,1,0:T(8,128)(2,1)S(1)} %get-tuple-element.21.probs, f32[4,32,128]{2,1,0:T(8,128)S(1)} %get-tuple-element.22.base, bf16[4,1,2,4096,128]{4,3,2,1,0:T(8,128)(2,1)} %values.1), custom_call_target="tpu_custom_call" | custom-call | flops 134217728 | bytes 4194304 | tf_op jit(solution)/shard_map/mix/pallas_call | solution.py:251
  72.0 5.0 %all-to-all-done.2 = f32[128,1,128]{2,1,0:T(1,128)S(1)} async-done(((f32[128,1,128]{2,1,0:T(1,128)}), f32[128,1,128]{2,1,0:T(1,128)S(1)}, u32[]{:S(2)}, u32[]{:S(2)}) %all-to-all-start.2) | async-done | bytes 65568 | tf_op jit(solution)/shard_map/all_to_all | solution.py:333
  77.1 1.0 %ratios.1 = (f32[4,4]{1,0:T(4,128)}, f32[4]{0:T(128)}) custom-call(f32[128,128]{1,0:T(8,128)S(1)} %bitcast.34), custom_call_target="tpu_custom_call" | custom-call | tf_op jit(solution)/shard_map/ratios/pallas_call | solution.py:293
  (8 shorter events, 0.2 us)
Async XLA Ops:
  1.7 8.2 %collective-permute-start = (bf16[1,8,16,512]{3,2,1,0:T(8,128)(2,1)S(1)}, bf16[1,8,16,512]{3,2,1,0:T(8,128)(2,1)S(1)}, u32[]{:S(2)}, u32[]{:S(2)}) collective-permute-start(bf16[1,8,16,512]{3,2,1,0:T(8,128)(2,1)S(1)} %get-tuple-element.33), channel_id=1, source_target_pairs={{0,64},{8,72},{16,80},{24,88},{32,96},{40,104},{48,112},{56,120},{... | collective-permute-start | bytes 393224 | tf_op jit(solution)/shard_map/ppermute | solution.py:319
  10.0 8.2 %collective-permute-start.1 = (bf16[2,4,16,512]{3,2,1,0:T(8,128)(2,1)S(1)}, bf16[2,4,16,512]{3,2,1,0:T(8,128)(2,1)S(1)}, u32[]{:S(2)}, u32[]{:S(2)}) collective-permute-start(bf16[2,4,16,512]{3,2,1,0:T(8,128)(2,1)S(1)} %get-tuple-element.31), channel_id=1, source_target_pairs={{0,8},{8,0},{16,24},{24,16},{32,40},{40,32},{48,56},{56,48},{64,72... | collective-permute-start | bytes 393224 | tf_op jit(solution)/shard_map/ppermute | solution.py:319
  11.0 25.0 %all-to-all-start = ((bf16[8,64,1280]{2,1,0:T(8,128)(2,1)}), bf16[8,64,1280]{2,1,0:T(8,128)(2,1)S(1)}, u32[]{:S(2)}, u32[]{:S(2)}) async-start(bf16[8,64,1280]{2,1,0:T(8,128)(2,1)} %get-tuple-element.19), calls=%async_computation | async-start | bytes 2621440 | tf_op jit(solution)/shard_map/all_to_all | solution.py:324
  18.3 4.9 %collective-permute-start.2 = (bf16[4,2,16,512]{3,2,0,1:T(8,128)(2,1)S(1)}, bf16[4,2,16,512]{3,2,0,1:T(8,128)(2,1)S(1)}, u32[]{:S(2)}, u32[]{:S(2)}) collective-permute-start(bf16[4,2,16,512]{3,2,0,1:T(8,128)(2,1)S(1)} %get-tuple-element.29), channel_id=1, source_target_pairs={{0,16},{8,24},{16,0},{24,8},{32,48},{40,56},{48,32},{56,40},{64,80... | collective-permute-start | bytes 393224 | tf_op jit(solution)/shard_map/ppermute | solution.py:319
  23.2 5.5 %collective-permute-start.3 = (bf16[8,1,16,512]{3,2,0,1:T(8,128)(2,1)S(1)}, bf16[8,1,16,512]{3,2,0,1:T(8,128)(2,1)S(1)}, u32[]{:S(2)}, u32[]{:S(2)}) collective-permute-start(bf16[8,1,16,512]{3,2,0,1:T(8,128)(2,1)S(1)} %get-tuple-element.27), channel_id=1, source_target_pairs={{0,48},{8,56},{16,32},{24,40},{32,16},{40,24},{48,0},{56,8},{64,11... | collective-permute-start | bytes 393224 | tf_op jit(solution)/shard_map/ppermute | solution.py:319
  36.4 3.0 %collective-permute-start.4 = (f32[128,1280]{1,0:T(8,128)S(1)}, f32[128,1280]{1,0:T(8,128)S(1)}, u32[]{:S(2)}, u32[]{:S(2)}) collective-permute-start(f32[128,1280]{1,0:T(8,128)S(1)} %product.3), channel_id=1, source_target_pairs={{0,8},{8,0},{16,24},{24,16},{32,40},{40,32},{48,56},{56,48},{64,72... | collective-permute-start | bytes 1966088 | tf_op jit(solution)/shard_map/ppermute | solution.py:327
  54.0 3.4 %copy-start = (bf16[4,1,2,4096,128]{4,3,2,1,0:T(8,128)(2,1)S(1)}, bf16[4,1,2,4096,128]{4,3,2,1,0:T(8,128)(2,1)}, u32[]{:S(2)}) copy-start(bf16[4,1,2,4096,128]{4,3,2,1,0:T(8,128)(2,1)} %values.1) | copy-start | bytes 25165828
  60.7 16.4 %all-to-all-start.2 = ((f32[128,1,128]{2,1,0:T(1,128)}), f32[128,1,128]{2,1,0:T(1,128)S(1)}, u32[]{:S(2)}, u32[]{:S(2)}) async-start(f32[128,1,128]{2,1,0:T(1,128)} %bitcast.18), calls=%async_computation.2 | async-start | bytes 131072 | tf_op jit(solution)/shard_map/all_to_all | solution.py:333

commit v3 on v2

--- a/solution.py
+++ b/solution.py
@@ -20,11 +20,11 @@
 in_vmem = functools.partial(pltpu.with_memory_space_constraint, memory_space=pltpu.VMEM)
 LOG2E = 1.4426950408889634
 AHEAD = 3
-HOPS = (8, 1, 2, 6)
-
-
-def adam_kernel(master, moment, second, grad, new, weights, a, b, c, g, n, w, arrive, leave):
-    parts, rows, width = w.shape
+HOPS = ((0, 8), (0, 2, 4, 6), (0, 1))
+
+
+def adam_kernel(master, moment, second, grad, out, a, b, c, g, n, arrive, leave):
+    parts, rows, width = n.shape
     sources = ((master, a), (moment, b), (second, c), (grad, g))
 
     def columns(i):
@@ -36,11 +36,9 @@
             for k, (hbm, buf) in enumerate(sources)
         ]
 
-    def stores(i):
-        return [
-            pltpu.make_async_copy(n.at[i], new.at[:, columns(i)], leave.at[i, 0]),
-            pltpu.make_async_copy(w.at[i], weights.at[i], leave.at[i, 1]),
-        ]
+    def store(i):
+        to = out.at[i] if len(out.shape) == 3 else out.at[:, columns(i)]
+        return pltpu.make_async_copy(n.at[i], to, leave.at[i])
 
     for i in range(AHEAD):
         for copy in fetches(i):
@@ -59,52 +57,42 @@
             fresh_second = 0.95 * c[i, at] + 0.05 * gradient * gradient
             spread = jnp.sqrt(fresh_second * (1.0 / (1.0 - 0.95**10))) + 1e-08
             fresh = a[i, at] - (0.005 / (1.0 - 0.9**10)) * fresh_moment / spread
-            n[i, at] = fresh
-            w[i, at] = fresh.astype(BF16)
+            n[i, at] = fresh.astype(n.dtype)
             return carry
 
         lax.fori_loop(0, rows // 16, tile, 0)
-        for copy in stores(i):
-            copy.start()
+        store(i).start()
     for i in range(parts):
-        for copy in stores(i):
-            copy.wait()
-
-
-def adam(master, moment, second, grad, parts):
-    rows, columns = master.shape
+        store(i).wait()
+
+
+def adam(arrays, parts, shape, kind, name):
+    rows, columns = arrays[0].shape
     width = columns // parts
+    kinds = [x.dtype for x in arrays] + [kind]
     return pl.pallas_call(
         adam_kernel,
         in_specs=[ANY] * 4,
-        out_specs=[ANY] * 2,
-        out_shape=[
-            jax.ShapeDtypeStruct((rows, columns), F32),
-            jax.ShapeDtypeStruct((parts, rows, width), BF16),
-        ],
+        out_specs=ANY,
+        out_shape=jax.ShapeDtypeStruct(shape, kind),
         scratch_shapes=[
-            pltpu.VMEM((parts, rows, width), F32),
-            pltpu.VMEM((parts, rows, width), F32),
-            pltpu.VMEM((parts, rows, width), F32),
-            pltpu.VMEM((parts, rows, width), BF16),
-            pltpu.VMEM((parts, rows, width), F32),
-            pltpu.VMEM((parts, rows, width), BF16),
+            *(pltpu.VMEM((parts, rows, width), k) for k in kinds),
             pltpu.SemaphoreType.DMA((parts, 4)),
-            pltpu.SemaphoreType.DMA((parts, 2)),
+            pltpu.SemaphoreType.DMA((parts,)),
         ],
         compiler_params=pltpu.CompilerParams(vmem_limit_bytes=60 * MIB),
         cost_estimate=pl.CostEstimate(
-            flops=12 * rows * columns, bytes_accessed=20 * rows * columns, transcendentals=0
+            flops=12 * rows * columns, bytes_accessed=18 * rows * columns, transcendentals=0
         ),
-        name="adam",
-    )(master, moment, second, grad)
+        name=name,
+    )(*arrays)
 
 
 def offset(i):
     total = 0
-    for k, hop in enumerate(HOPS):
-        if i >> (len(HOPS) - 1 - k) & 1:
-            total ^= hop
+    for hops in reversed(HOPS):
+        total ^= hops[i % len(hops)]
+        i //= len(hops)
     return total
 
 
@@ -143,40 +131,64 @@
     )(in_hbm(lengths), in_hbm(versions), in_hbm(recorded), in_hbm(hidden))
 
 
-def product_kernel(flip, spread, weights, out):
+def product_kernel(flip, spread, weights, *rest):
+    keys = None
+    if flip:
+        _, out = rest
+    else:
+        cache, out, keys, sems = rest
+        copies = [
+            pltpu.make_async_copy(cache.at[r, 0, 0], keys.at[r], sems.at[r])
+            for r in range(keys.shape[0])
+        ]
+        for copy in copies:
+            copy.start()
     me = lax.axis_index("fsdp")
     chips = out.shape[0] // spread.shape[1]
-    where = {offset(i): i for i in range(spread.shape[0])}
     blocks = []
     for chip in range(chips):
         away = me ^ flip ^ (2 * chip + (me & 1))
         at = jnp.int32(0)
-        for far, i in where.items():
-            at = jnp.where(away == far, i, at)
+        for i in range(spread.shape[0]):
+            at = jnp.where(away == offset(i), i, at)
         blocks.append(spread[at])
     out[...] = jnp.dot(
         jnp.concatenate(blocks, axis=0), weights[...], preferred_element_type=F32
     )
-
-
-def product(spread, weights, n_fsdp, flip):
+    if not flip:
+        for copy in copies:
+            copy.wait()
+
+
+def product(spread, weights, n_fsdp, flip, after=None, cache=None):
     _, tall, depth = spread.shape
     width = weights.shape[1]
+    partial = jax.ShapeDtypeStruct((n_fsdp // 2 * tall, width), F32)
+    if flip:
+        extra = dict(in_specs=[VMEM] * 2 + [ANY], out_specs=VMEM, out_shape=partial)
+        operands = (in_hbm(after),)
+    else:
+        rows, _, _, slots, _ = cache.shape
+        extra = dict(
+            in_specs=[VMEM] * 2 + [ANY],
+            out_specs=[VMEM] * 2,
+            out_shape=[partial, pltpu.VMEM((rows, slots, HD), BF16)],
+            scratch_shapes=[pltpu.SemaphoreType.DMA((rows,))],
+        )
+        operands = (in_hbm(cache),)
     return pl.pallas_call(
         functools.partial(product_kernel, flip),
-        in_specs=[VMEM] * 2,
-        out_specs=VMEM,
-        out_shape=jax.ShapeDtypeStruct((n_fsdp // 2 * tall, width), F32),
         compiler_params=pltpu.CompilerParams(vmem_limit_bytes=16 * MIB),
         cost_estimate=pl.CostEstimate(
-            flops=n_fsdp * tall * depth * width, bytes_accessed=16 * MIB, transcendentals=0
+            flops=n_fsdp * tall * depth * width, bytes_accessed=2 * MIB, transcendentals=0
         ),
         name="product",
-    )(spread, weights)
-
-
-def score_kernel(steps, parts, cache, meta, probs, base, lse_out):
-    rows = cache.shape[0]
+        **extra,
+    )(spread, weights, *operands)
+
+
+def score_kernel(steps, parts, keys, meta, probs, base, lse_out):
+    rows = keys.shape[0]
     heads = parts.shape[2] // HD - 2
     total = parts[0]
     for i in range(1, parts.shape[0]):
@@ -191,7 +203,7 @@
         ).astype(BF16)
         new_keys = mine[:, heads * HD : (heads + 1) * HD].astype(BF16)
         new_values = mine[:, (heads + 1) * HD :].astype(BF16)
-        old = lax.dot_general(queries, cache[r, 0, 0], contract, preferred_element_type=F32)
+        old = lax.dot_general(queries, keys[r], contract, preferred_element_type=F32)
         slot = lax.broadcasted_iota(jnp.int32, old.shape, 1).astype(F32)
         old = jnp.where(slot < meta[r + 1 : r + 2, 0:1], old, -1e31)
         new = lax.dot_general(queries, new_keys, contract, preferred_element_type=F32)
@@ -214,8 +226,8 @@
     lse_out[...] = jnp.broadcast_to(line, lse_out.shape)
 
 
-def score(parts, cache, meta, steps, copies):
-    rows, _, _, slots, _ = cache.shape
+def score(parts, keys, meta, steps, copies):
+    rows, slots, _ = keys.shape
     heads = parts.shape[2] // HD - 2
     return pl.pallas_call(
         functools.partial(score_kernel, steps),
@@ -229,11 +241,11 @@
         compiler_params=pltpu.CompilerParams(vmem_limit_bytes=24 * MIB),
         cost_estimate=pl.CostEstimate(
             flops=2 * rows * heads * steps * slots * HD,
-            bytes_accessed=cache.size,
+            bytes_accessed=2 * keys.size,
             transcendentals=rows * heads * steps * slots,
         ),
         name="score",
-    )(parts, in_vmem(cache), meta)
+    )(parts, in_vmem(keys), meta)
 
 
 def mix_kernel(steps, probs, base, values, out):
@@ -310,26 +322,33 @@
     depth = width // n_fsdp
     chips = n_fsdp // 2
     cores = [[i for i in range(n_fsdp) if i % 2 == c] for c in range(2)]
-    pairs = [(i, i ^ 1) for i in range(n_fsdp)]
+
+    def move(block, hop):
+        return lax.ppermute(block, "fsdp", [(i, i ^ hop) for i in range(n_fsdp)]) if hop else block
 
     meta, spread = stage(lengths, versions, recorded, hidden, n_fsdp)
-    new_master, fresh = adam(master, moment, second, grad, n_tp)
-    for k, hop in enumerate(HOPS):
-        halves = spread.reshape(2**k, 2, -1, tall, depth)
-        moved = lax.ppermute(halves[:, 1], "fsdp", [(i, i ^ hop) for i in range(n_fsdp)])
-        if k == 0:
-            moved, fresh = lax.optimization_barrier((moved, fresh))
-        spread = jnp.stack([halves[:, 0], moved], axis=1)
+    spread = spread.reshape(*(len(hops) for hops in HOPS), tall, depth)
+    along_x = [move(spread[k], hop) for k, hop in enumerate(HOPS[0])]
+
+    learned = (master, moment, second, grad)
+    fresh = adam(learned, n_tp, (n_tp, master.shape[0], master.shape[1] // n_tp), BF16, "weights")
+    fresh, along_x, learned = lax.optimization_barrier((fresh, along_x, learned))
+    weights = lax.all_to_all(fresh, "tp", 0, 0, tiled=True).reshape(depth, -1)
+    new_master = adam(learned, n_tp, master.shape, F32, "master")
+
+    spread = jnp.stack(along_x)
+    spread = jnp.stack([move(spread[:, k], hop) for k, hop in enumerate(HOPS[1])], axis=1)
+    spread = jnp.stack([move(spread[:, :, k], hop) for k, hop in enumerate(HOPS[2])], axis=2)
     spread = spread.reshape(n_fsdp, tall, depth)
-    weights = lax.all_to_all(fresh, "tp", 0, 0, tiled=True).reshape(depth, -1)
-
-    sent = product(spread, weights, n_fsdp, 1)
-    arrived = lax.ppermute(sent, "fsdp", pairs)
-    partial = product(spread, weights, n_fsdp, 0) + arrived
+
+    sent = product(spread, weights, n_fsdp, 1, after=new_master)
+    arrived = move(sent, 1)
+    partial, keys = product(spread, weights, n_fsdp, 0, cache=cache)
+    partial = partial + arrived
     parts = lax.all_to_all(
         partial.reshape(chips, tall, -1), "fsdp", 0, 0, tiled=True, axis_index_groups=cores
     )
-    probs, base, lines = score(parts, cache, meta, steps, n_fsdp * n_tp)
+    probs, base, lines = score(parts, keys, meta, steps, n_fsdp * n_tp)
     lines = lax.all_to_all(lines, ("fsdp", "tp"), 0, 0, tiled=True)
     attention = mix(probs, base, cache, steps)
     ratios, version_means = final(lines, rows, steps)

time: 78.5 us -> 74.2 us (0.945)
  waiting for transfers between devices: 19.7 us -> 9.37 us
  Pallas kernels: 16.6 us -> 23.7 us
  local copies, waits for them, and re-layouts: 3.46 us -> 0.04 us
  starting transfers between devices: 22.8 us -> 25.1 us
    all_to_all x1, waiting for transfers between devices: 7.24 us -> 0.01 us  [shards(): weights = lax.all_to_all(fresh, 'tp', 0, 0, tiled=True).reshape(depth, -1)]
    pallas_call x3 -> x4, Pallas kernels: 6.87 us -> 14 us  [the longest x2 11.1 us: adam(): pl.pallas_call(adam_kernel, in_specs=[ANY] * 4, out_specs=ANY, out_shape=...]
    unnamed x2 -> x0, local copies, waits for them, and re-layouts: 3.38 us -> none
    ppermute x5 -> x6, waiting for transfers between devices: 7.49 us -> 4.35 us  [move(): lax.ppermute(block, 'fsdp', [(i, i ^ hop) for i in range(n_fsdp)])]
    ppermute x5 -> x6, starting transfers between devices: 8.61 us -> 11.3 us  [move(): lax.ppermute(block, 'fsdp', [(i, i ^ hop) for i in range(n_fsdp)])]
  transfers between devices with their start and end apart: 7 -> 8, of which waited for: 5 -> 3; matrix products, arithmetic and copies ran while one was open for 0% -> 0% of each run, Pallas kernels for 14% -> 24%
where the time goes in v3:
time: 74.2 us; the launch traced here: 73.8 us
  starting transfers between devices  25.1 us (34%)
  Pallas kernels  23.7 us (32%)
  blocking collectives  14.7 us (20%)
  waiting for transfers between devices  9.37 us (13%)
  between operations  0.75 us (1%)
    all_to_all x1, blocking collectives, shards(): lax.all_to_all(partial.reshape(chips, tall, -1), 'fsdp', 0, 0, tiled=True...  14.7 us
    ppermute x6, starting transfers between devices, move(): lax.ppermute(block, 'fsdp', [(i, i ^ hop) for i in range(n_fsdp)])  11.3 us
    pallas_call x2, Pallas kernels, adam(): pl.pallas_call(adam_kernel, in_specs=[ANY] * 4, out_specs=ANY, out_shape=...  11.1 us
    all_to_all x1, starting transfers between devices, shards(): weights = lax.all_to_all(fresh, 'tp', 0, 0, tiled=True).reshape(depth, -1)  7.21 us
    all_to_all x1, starting transfers between devices, shards(): lines = lax.all_to_all(lines, ('fsdp', 'tp'), 0, 0, tiled=True)  6.61 us
    all_to_all x1, waiting for transfers between devices, shards(): lines = lax.all_to_all(lines, ('fsdp', 'tp'), 0, 0, tiled=True)  5.02 us
    ppermute x6, waiting for transfers between devices, move(): lax.ppermute(block, 'fsdp', [(i, i ^ hop) for i in range(n_fsdp)])  4.35 us
    pallas_call x1, Pallas kernels, mix(): pl.pallas_call(functools.partial(mix_kernel, steps), grid=(rows,), in_spe...  4.3 us
  transfers between devices with their start and end apart: 8, of which 3 were waited for; matrix products, arithmetic and copies ran while one was open for 0% of the time, Pallas kernels for 24%

profile of v3, /device:TPU:1, one launch (start us, length us, event | category | flops | bytes accessed | tf_op | source)
XLA Modules:
  0.0 73.8 jit_solution(13194957758914917954)
XLA Ops:
  0.6 1.0 %stage.1 = (f32[8,128]{1,0:T(8,128)S(1)}, bf16[16,16,512]{2,1,0:T(8,128)(2,1)S(1)}) custom-call(s32[4]{0:T(128)} %lengths.1, s32[4]{0:T(128)} %versions.1, f32[4,4]{1,0:T(4,128)} %recorded.1, bf16[4,4,8192]{2,1,0:T(4,128)(2,1)} %hidden.1), custom_call_target="tpu_custom_call" | custom-call | tf_op jit(solution)/shard_map/stage/pallas_call | solution.py:121
  1.7 2.1 %collective-permute-start = (bf16[4,2,16,512]{3,2,1,0:T(8,128)(2,1)S(1)}, bf16[4,2,16,512]{3,2,1,0:T(8,128)(2,1)S(1)}, u32[]{:S(2)}, u32[]{:S(2)}) collective-permute-start(bf16[4,2,16,512]{3,2,1,0:T(8,128)(2,1)S(1)} %bitcast.39), channel_id=1, source_target_pairs={{0,64},{8,72},{16,80},{24,88},{32,96},{40,104},{48,112},{56,120},{... | collective-permute-start | bytes 393224 | tf_op jit(solution)/shard_map/ppermute | solution.py:327
  3.8 5.5 %weights.1 = bf16[8,64,1280]{2,1,0:T(8,128)(2,1)} custom-call(f32[64,10240]{1,0:T(8,128)} %master.4, f32[64,10240]{1,0:T(8,128)} %moment.2, f32[64,10240]{1,0:T(8,128)} %second.2, bf16[64,10240]{1,0:T(8,128)(2,1)} %grad.2), custom_call_target="tpu_custom_call" | custom-call | flops 7864320 | bytes 11796480 | tf_op jit(solution)/shard_map/weights/pallas_call | solution.py:73
  9.3 0.0 collective-permute-done
  9.3 7.2 %all-to-all-start = ((bf16[8,64,1280]{2,1,0:T(8,128)(2,1)}), bf16[8,64,1280]{2,1,0:T(8,128)(2,1)S(1)}, u32[]{:S(2)}, u32[]{:S(2)}) async-start(bf16[8,64,1280]{2,1,0:T(8,128)(2,1)} %weights.1), calls=%async_computation | async-start | bytes 2621440 | tf_op jit(solution)/shard_map/all_to_all | solution.py:336
  16.6 1.4 %collective-permute-start.1 = (bf16[2,2,16,512]{3,2,0,1:T(8,128)(2,1)S(1)}, bf16[2,2,16,512]{3,2,0,1:T(8,128)(2,1)S(1)}, u32[]{:S(2)}, u32[]{:S(2)}) collective-permute-start(bf16[2,2,16,512]{3,2,0,1:T(8,128)(2,1)S(1)} %get-tuple-element.39), channel_id=1, source_target_pairs={{0,16},{8,24},{16,0},{24,8},{32,48},{40,56},{48,32},{56,40},{64,80... | collective-permute-start | bytes 196616 | tf_op jit(solution)/shard_map/ppermute | solution.py:327
  17.9 1.9 %collective-permute-start.3 = (bf16[2,2,16,512]{3,2,0,1:T(8,128)(2,1)S(1)}, bf16[2,2,16,512]{3,2,0,1:T(8,128)(2,1)S(1)}, u32[]{:S(2)}, u32[]{:S(2)}) collective-permute-start(bf16[2,2,16,512]{3,2,0,1:T(8,128)(2,1)S(1)} %get-tuple-element.40), channel_id=1, source_target_pairs={{0,48},{8,56},{16,32},{24,40},{32,16},{40,24},{48,0},{56,8},{64,11... | collective-permute-start | bytes 196616 | tf_op jit(solution)/shard_map/ppermute | solution.py:327
  19.8 0.7 collective-permute-start.2
  20.6 0.0 collective-permute-done.1
  20.6 1.7 %collective-permute-done.3 = bf16[2,2,16,512]{3,2,0,1:T(8,128)(2,1)S(1)} collective-permute-done((bf16[2,2,16,512]{3,2,0,1:T(8,128)(2,1)S(1)}, bf16[2,2,16,512]{3,2,0,1:T(8,128)(2,1)S(1)}, u32[]{:S(2)}, u32[]{:S(2)}) %collective-permute-start.3) | collective-permute-done | bytes 65568 | tf_op jit(solution)/shard_map/ppermute | solution.py:327
  22.3 2.6 %collective-permute-done.2 = bf16[2,2,16,512]{3,2,0,1:T(8,128)(2,1)S(1)} collective-permute-done((bf16[2,2,16,512]{3,2,0,1:T(8,128)(2,1)S(1)}, bf16[2,2,16,512]{3,2,0,1:T(8,128)(2,1)S(1)}, u32[]{:S(2)}, u32[]{:S(2)}) %collective-permute-start.2) | collective-permute-done | bytes 65568 | tf_op jit(solution)/shard_map/ppermute | solution.py:327
  25.0 2.6 %collective-permute-start.4 = (bf16[2,4,16,512]{3,2,1,0:T(8,128)(2,1)S(1)}, bf16[2,4,16,512]{3,2,1,0:T(8,128)(2,1)S(1)}, u32[]{:S(2)}, u32[]{:S(2)}) collective-permute-start(bf16[2,4,16,512]{3,2,1,0:T(8,128)(2,1)S(1)} %get-tuple-element.37), channel_id=1, source_target_pairs={{0,8},{8,0},{16,24},{24,16},{32,40},{40,32},{48,56},{56,48},{64,72... | collective-permute-start | bytes 393224 | tf_op jit(solution)/shard_map/ppermute | solution.py:327
  27.5 5.7 %master.3.rest_0_ = f32[64,10240]{1,0:T(8,128)} custom-call(f32[64,10240]{1,0:T(8,128)} %master.4, f32[64,10240]{1,0:T(8,128)} %moment.2, f32[64,10240]{1,0:T(8,128)} %second.2, bf16[64,10240]{1,0:T(8,128)(2,1)} %grad.2), custom_call_target="tpu_custom_call" | custom-call | flops 7864320 | bytes 11796480 | tf_op jit(solution)/shard_map/master/pallas_call | solution.py:73
  33.2 0.0 collective-permute-done.4
  33.3 0.0 all-to-all-done
  33.3 0.4 product.3
  33.7 2.6 %collective-permute-start.5 = (f32[128,1280]{1,0:T(8,128)S(1)}, f32[128,1280]{1,0:T(8,128)S(1)}, u32[]{:S(2)}, u32[]{:S(2)}) collective-permute-start(f32[128,1280]{1,0:T(8,128)S(1)} %product.3), channel_id=1, source_target_pairs={{0,8},{8,0},{16,24},{24,16},{32,40},{40,32},{48,56},{56,48},{64,72... | collective-permute-start | bytes 1966088 | tf_op jit(solution)/shard_map/ppermute | solution.py:327
  36.2 2.5 %product.2 = (f32[128,1280]{1,0:T(8,128)S(1)}, bf16[4,4096,128]{2,1,0:T(8,128)(2,1)S(1)}) custom-call(bf16[16,16,512]{2,1,0:T(8,128)(2,1)S(1)} %bitcast.34, bf16[512,1280]{1,0:T(8,128)(2,1)S(1)} %bitcast.32, bf16[4,1,2,4096,128]{4,3,2,1,0:T(8,128)(2,1)} %values.1), custom_call_target="tpu_custom_call" | custom-call | flops 167772160 | bytes 2097152 | tf_op jit(solution)/shard_map/product/pallas_call | solution.py:179
  38.7 0.0 collective-permute-done.5
  38.7 0.1 add.3
  38.8 14.7 %all_to_all.21.parts = f32[8,16,1280]{2,1,0:T(8,128)S(1)} all-to-all(f32[8,16,1280]{2,1,0:T(8,128)S(1)} %bitcast.36), channel_id=1, replica_groups={{0,16,32,48,64,80,96,112},{8,24,40,56,72,88,104,120},{1,17,33,49,65,81,..., dimensions={0} | all-to-all | bytes 1310720 | tf_op jit(solution)/shard_map/all_to_all | solution.py:348
  53.5 3.3 %score.1 = (bf16[4,32,4096]{2,1,0:T(8,128)(2,1)S(1)}, f32[4,32,128]{2,1,0:T(8,128)S(1)}, f32[128,128]{1,0:T(8,128)}) custom-call(f32[8,16,1280]{2,1,0:T(8,128)S(1)} %all_to_all.21.parts, bf16[4,4096,128]{2,1,0:T(8,128)(2,1)S(1)} %get-tuple-element.29.keys, f32[8,128]{1,0:T(8,128)S(1)} %get-tuple-element.30.meta), custom_call_target="tpu_custom_call" | custom-call | flops 134217728 | bytes 4194304 | tf_op jit(solution)/shard_map/score/pallas_call | solution.py:232
  56.8 6.6 %all-to-all-start.2 = ((f32[128,1,128]{2,1,0:T(1,128)}), f32[128,1,128]{2,1,0:T(1,128)S(1)}, u32[]{:S(2)}, u32[]{:S(2)}) async-start(f32[128,1,128]{2,1,0:T(1,128)} %bitcast.20), calls=%async_computation.2 | async-start | bytes 131072 | tf_op jit(solution)/shard_map/all_to_all | solution.py:352
  63.4 4.3 %mix.1 = bf16[4,4,1024]{2,1,0:T(4,128)(2,1)} custom-call(bf16[4,32,4096]{2,1,0:T(8,128)(2,1)S(1)} %get-tuple-element.31.probs, f32[4,32,128]{2,1,0:T(8,128)S(1)} %get-tuple-element.32.base, bf16[4,1,2,4096,128]{4,3,2,1,0:T(8,128)(2,1)} %values.1), custom_call_target="tpu_custom_call" | custom-call | flops 134217728 | bytes 4194304 | tf_op jit(solution)/shard_map/mix/pallas_call | solution.py:263
  67.7 5.0 %all-to-all-done.2 = f32[128,1,128]{2,1,0:T(1,128)S(1)} async-done(((f32[128,1,128]{2,1,0:T(1,128)}), f32[128,1,128]{2,1,0:T(1,128)S(1)}, u32[]{:S(2)}, u32[]{:S(2)}) %all-to-all-start.2) | async-done | bytes 65568 | tf_op jit(solution)/shard_map/all_to_all | solution.py:352
  72.7 1.0 %ratios.1 = (f32[4,4]{1,0:T(4,128)}, f32[4]{0:T(128)}) custom-call(f32[128,128]{1,0:T(8,128)S(1)} %bitcast.35), custom_call_target="tpu_custom_call" | custom-call | tf_op jit(solution)/shard_map/ratios/pallas_call | solution.py:305
  (5 shorter events, 0.1 us)
Async XLA Ops:
  1.7 7.6 %collective-permute-start = (bf16[4,2,16,512]{3,2,1,0:T(8,128)(2,1)S(1)}, bf16[4,2,16,512]{3,2,1,0:T(8,128)(2,1)S(1)}, u32[]{:S(2)}, u32[]{:S(2)}) collective-permute-start(bf16[4,2,16,512]{3,2,1,0:T(8,128)(2,1)S(1)} %bitcast.39), channel_id=1, source_target_pairs={{0,64},{8,72},{16,80},{24,88},{32,96},{40,104},{48,112},{56,120},{... | collective-permute-start | bytes 393224 | tf_op jit(solution)/shard_map/ppermute | solution.py:327
  9.3 24.0 %all-to-all-start = ((bf16[8,64,1280]{2,1,0:T(8,128)(2,1)}), bf16[8,64,1280]{2,1,0:T(8,128)(2,1)S(1)}, u32[]{:S(2)}, u32[]{:S(2)}) async-start(bf16[8,64,1280]{2,1,0:T(8,128)(2,1)} %weights.1), calls=%async_computation | async-start | bytes 2621440 | tf_op jit(solution)/shard_map/all_to_all | solution.py:336
  16.6 4.0 %collective-permute-start.1 = (bf16[2,2,16,512]{3,2,0,1:T(8,128)(2,1)S(1)}, bf16[2,2,16,512]{3,2,0,1:T(8,128)(2,1)S(1)}, u32[]{:S(2)}, u32[]{:S(2)}) collective-permute-start(bf16[2,2,16,512]{3,2,0,1:T(8,128)(2,1)S(1)} %get-tuple-element.39), channel_id=1, source_target_pairs={{0,16},{8,24},{16,0},{24,8},{32,48},{40,56},{48,32},{56,40},{64,80... | collective-permute-start | bytes 196616 | tf_op jit(solution)/shard_map/ppermute | solution.py:327
  17.9 4.3 %collective-permute-start.3 = (bf16[2,2,16,512]{3,2,0,1:T(8,128)(2,1)S(1)}, bf16[2,2,16,512]{3,2,0,1:T(8,128)(2,1)S(1)}, u32[]{:S(2)}, u32[]{:S(2)}) collective-permute-start(bf16[2,2,16,512]{3,2,0,1:T(8,128)(2,1)S(1)} %get-tuple-element.40), channel_id=1, source_target_pairs={{0,48},{8,56},{16,32},{24,40},{32,16},{40,24},{48,0},{56,8},{64,11... | collective-permute-start | bytes 196616 | tf_op jit(solution)/shard_map/ppermute | solution.py:327
  19.8 5.1 %collective-permute-start.2 = (bf16[2,2,16,512]{3,2,0,1:T(8,128)(2,1)S(1)}, bf16[2,2,16,512]{3,2,0,1:T(8,128)(2,1)S(1)}, u32[]{:S(2)}, u32[]{:S(2)}) collective-permute-start(bf16[2,2,16,512]{3,2,0,1:T(8,128)(2,1)S(1)} %get-tuple-element.41), channel_id=1, source_target_pairs={{0,32},{8,40},{16,48},{24,56},{32,0},{40,8},{48,16},{56,24},{64,96... | collective-permute-start | bytes 196616 | tf_op jit(solution)/shard_map/ppermute | solution.py:327
  25.0 8.3 %collective-permute-start.4 = (bf16[2,4,16,512]{3,2,1,0:T(8,128)(2,1)S(1)}, bf16[2,4,16,512]{3,2,1,0:T(8,128)(2,1)S(1)}, u32[]{:S(2)}, u32[]{:S(2)}) collective-permute-start(bf16[2,4,16,512]{3,2,1,0:T(8,128)(2,1)S(1)} %get-tuple-element.37), channel_id=1, source_target_pairs={{0,8},{8,0},{16,24},{24,16},{32,40},{40,32},{48,56},{56,48},{64,72... | collective-permute-start | bytes 393224 | tf_op jit(solution)/shard_map/ppermute | solution.py:327
  33.7 5.0 %collective-permute-start.5 = (f32[128,1280]{1,0:T(8,128)S(1)}, f32[128,1280]{1,0:T(8,128)S(1)}, u32[]{:S(2)}, u32[]{:S(2)}) collective-permute-start(f32[128,1280]{1,0:T(8,128)S(1)} %product.3), channel_id=1, source_target_pairs={{0,8},{8,0},{16,24},{24,16},{32,40},{40,32},{48,56},{56,48},{64,72... | collective-permute-start | bytes 1966088 | tf_op jit(solution)/shard_map/ppermute | solution.py:327
  56.8 15.9 %all-to-all-start.2 = ((f32[128,1,128]{2,1,0:T(1,128)}), f32[128,1,128]{2,1,0:T(1,128)S(1)}, u32[]{:S(2)}, u32[]{:S(2)}) async-start(f32[128,1,128]{2,1,0:T(1,128)} %bitcast.20), calls=%async_computation.2 | async-start | bytes 131072 | tf_op jit(solution)/shard_map/all_to_all | solution.py:352

commit v4 on v3

--- a/solution.py
+++ b/solution.py
@@ -19,7 +19,7 @@
 in_hbm = functools.partial(pltpu.with_memory_space_constraint, memory_space=pltpu.HBM)
 in_vmem = functools.partial(pltpu.with_memory_space_constraint, memory_space=pltpu.VMEM)
 LOG2E = 1.4426950408889634
-AHEAD = 3
+AHEAD = 8
 HOPS = ((0, 8), (0, 2, 4, 6), (0, 1))
 
 
@@ -134,7 +134,7 @@
 def product_kernel(flip, spread, weights, *rest):
     keys = None
     if flip:
-        _, out = rest
+        (out,) = rest
     else:
         cache, out, keys, sems = rest
         copies = [
@@ -160,20 +160,20 @@
             copy.wait()
 
 
-def product(spread, weights, n_fsdp, flip, after=None, cache=None):
+def product(spread, weights, n_fsdp, flip, cache=None):
     _, tall, depth = spread.shape
     width = weights.shape[1]
     partial = jax.ShapeDtypeStruct((n_fsdp // 2 * tall, width), F32)
     if flip:
-        extra = dict(in_specs=[VMEM] * 2 + [ANY], out_specs=VMEM, out_shape=partial)
-        operands = (in_hbm(after),)
+        extra = dict(in_specs=[VMEM] * 2, out_specs=VMEM, out_shape=partial)
+        operands = ()
     else:
         rows, _, _, slots, _ = cache.shape
         extra = dict(
             in_specs=[VMEM] * 2 + [ANY],
             out_specs=[VMEM] * 2,
-            out_shape=[partial, pltpu.VMEM((rows, slots, HD), BF16)],
-            scratch_shapes=[pltpu.SemaphoreType.DMA((rows,))],
+            out_shape=[partial, pltpu.VMEM((rows - 1, slots, HD), BF16)],
+            scratch_shapes=[pltpu.SemaphoreType.DMA((rows - 1,))],
         )
         operands = (in_hbm(cache),)
     return pl.pallas_call(
@@ -187,29 +187,44 @@
     )(spread, weights, *operands)
 
 
-def score_kernel(steps, parts, keys, meta, probs, base, lse_out):
-    rows = keys.shape[0]
+def score_kernel(steps, parts, keys, cache, meta, probs, base, lse_out, last, p, arrive, leave):
+    rows = cache.shape[0]
     heads = parts.shape[2] // HD - 2
+    fetch = pltpu.make_async_copy(cache.at[rows - 1, 0, 0], last, arrive)
+    fetch.start()
     total = parts[0]
     for i in range(1, parts.shape[0]):
         total = total + parts[i]
     scale = HD ** (-0.5)
     contract = (((1,), (1,)), ((), ()))
-    line = meta[0:1]
-    for r in range(rows):
+
+    def scores(r):
         mine = total[r * steps : (r + 1) * steps]
         queries = jnp.concatenate(
             [mine[:, h * HD : (h + 1) * HD] for h in range(heads)], axis=0
         ).astype(BF16)
         new_keys = mine[:, heads * HD : (heads + 1) * HD].astype(BF16)
         new_values = mine[:, (heads + 1) * HD :].astype(BF16)
-        old = lax.dot_general(queries, keys[r], contract, preferred_element_type=F32)
+        if r == rows - 1:
+            fetch.wait()
+        old_keys = last[...] if r == rows - 1 else keys[r]
+        old = lax.dot_general(queries, old_keys, contract, preferred_element_type=F32)
         slot = lax.broadcasted_iota(jnp.int32, old.shape, 1).astype(F32)
         old = jnp.where(slot < meta[r + 1 : r + 2, 0:1], old, -1e31)
         new = lax.dot_general(queries, new_keys, contract, preferred_element_type=F32)
         step = lax.broadcasted_iota(jnp.int32, new.shape, 0) % steps
         later = lax.broadcasted_iota(jnp.int32, new.shape, 1)
-        new = jnp.where(later <= step, new, -1e31)
+        return old, jnp.where(later <= step, new, -1e31), new_values
+
+    def store(r):
+        return pltpu.make_async_copy(p.at[r], probs.at[r], leave.at[r])
+
+    line = meta[0:1]
+    following = scores(0)
+    for r in range(rows):
+        old, new, new_values = following
+        if r + 1 < rows:
+            following = scores(r + 1)
         top = jnp.maximum(
             jnp.max(old, axis=1, keepdims=True), jnp.max(new, axis=1, keepdims=True)
         )
@@ -218,34 +233,44 @@
         mass = jnp.sum(old, axis=1, keepdims=True) + jnp.sum(new, axis=1, keepdims=True)
         lse = top * scale + jnp.log(mass)
         inverse = 1.0 / mass
-        probs[r] = (old * inverse).astype(BF16)
+        p[r] = (old * inverse).astype(BF16)
+        store(r).start()
         base[r] = jnp.dot((new * inverse).astype(BF16), new_values, preferred_element_type=F32)
         place = lax.broadcasted_iota(jnp.int32, (heads * steps, 128), 0) % steps + r * steps
         lane = lax.broadcasted_iota(jnp.int32, (heads * steps, 128), 1)
         line = line + jnp.sum(jnp.where(place == lane, lse, 0.0), axis=0, keepdims=True)
     lse_out[...] = jnp.broadcast_to(line, lse_out.shape)
-
-
-def score(parts, keys, meta, steps, copies):
-    rows, slots, _ = keys.shape
+    for r in range(rows):
+        store(r).wait()
+
+
+def score(parts, keys, cache, meta, copies):
+    rows, _, _, slots, _ = cache.shape
     heads = parts.shape[2] // HD - 2
+    steps = parts.shape[1] // rows
     return pl.pallas_call(
         functools.partial(score_kernel, steps),
-        in_specs=[VMEM] * 3,
-        out_specs=[VMEM] * 3,
+        in_specs=[VMEM, VMEM, ANY, VMEM],
+        out_specs=[ANY, VMEM, VMEM],
         out_shape=[
             jax.ShapeDtypeStruct((rows, heads * steps, slots), BF16),
             jax.ShapeDtypeStruct((rows, heads * steps, HD), F32),
             jax.ShapeDtypeStruct((copies, 128), F32),
         ],
+        scratch_shapes=[
+            pltpu.VMEM((slots, HD), BF16),
+            pltpu.VMEM((rows, heads * steps, slots), BF16),
+            pltpu.SemaphoreType.DMA,
+            pltpu.SemaphoreType.DMA((rows,)),
+        ],
         compiler_params=pltpu.CompilerParams(vmem_limit_bytes=24 * MIB),
         cost_estimate=pl.CostEstimate(
             flops=2 * rows * heads * steps * slots * HD,
-            bytes_accessed=2 * keys.size,
+            bytes_accessed=cache.size,
             transcendentals=rows * heads * steps * slots,
         ),
         name="score",
-    )(parts, in_vmem(keys), meta)
+    )(parts, in_vmem(keys), in_hbm(cache), meta)
 
 
 def mix_kernel(steps, probs, base, values, out):
@@ -276,6 +301,10 @@
         ),
         name="mix",
     )(probs, base, in_hbm(cache))
+
+
+def total(x):
+    return jnp.sum(jnp.sum(x, axis=0, keepdims=True), axis=1, keepdims=True)
 
 
 def ratio_kernel(gathered, ratios, means):
@@ -289,10 +318,15 @@
     recorded = first[:, count : 2 * count]
     version = first[:, 2 * count : 3 * count]
     ratio = jnp.exp(jnp.clip(normalizer - recorded, -2.0, 2.0))
+    lane = lax.broadcasted_iota(jnp.int32, means.shape, 1)
+    sums = jnp.zeros(means.shape, F32)
+    members = jnp.zeros(means.shape, F32)
     for v in range(VERSIONS):
         hit = version == float(v)
-        members = jnp.sum(jnp.where(hit, 1.0, 0.0))
-        means[v] = jnp.sum(jnp.where(hit, ratio, 0.0)) / jnp.maximum(members, 1.0)
+        there = lane == v
+        sums = jnp.where(there, total(jnp.where(hit, ratio, 0.0)), sums)
+        members = jnp.where(there, total(jnp.where(hit, 1.0, 0.0)), members)
+    means[...] = sums / jnp.maximum(members, 1.0)
     group = lax.broadcasted_iota(jnp.int32, ratio.shape, 0)
     mine = jnp.sum(
         jnp.where(group == lax.axis_index("fsdp"), ratio, 0.0), axis=0, keepdims=True
@@ -305,10 +339,10 @@
     return pl.pallas_call(
         ratio_kernel,
         in_specs=[VMEM],
-        out_specs=[VMEM, SMEM],
+        out_specs=[VMEM, VMEM],
         out_shape=[
             jax.ShapeDtypeStruct((rows, steps), F32),
-            jax.ShapeDtypeStruct((VERSIONS,), F32),
+            jax.ShapeDtypeStruct((1, VERSIONS), F32),
         ],
         name="ratios",
     )(in_vmem(gathered))
@@ -337,22 +371,24 @@
     new_master = adam(learned, n_tp, master.shape, F32, "master")
 
     spread = jnp.stack(along_x)
-    spread = jnp.stack([move(spread[:, k], hop) for k, hop in enumerate(HOPS[1])], axis=1)
+    along_y = [move(spread[:, k], hop) for k, hop in enumerate(HOPS[1])]
+    along_y, new_master = lax.optimization_barrier((along_y, new_master))
+    spread = jnp.stack(along_y, axis=1)
     spread = jnp.stack([move(spread[:, :, k], hop) for k, hop in enumerate(HOPS[2])], axis=2)
     spread = spread.reshape(n_fsdp, tall, depth)
 
-    sent = product(spread, weights, n_fsdp, 1, after=new_master)
+    sent = product(spread, weights, n_fsdp, 1)
     arrived = move(sent, 1)
     partial, keys = product(spread, weights, n_fsdp, 0, cache=cache)
     partial = partial + arrived
     parts = lax.all_to_all(
         partial.reshape(chips, tall, -1), "fsdp", 0, 0, tiled=True, axis_index_groups=cores
     )
-    probs, base, lines = score(parts, keys, meta, steps, n_fsdp * n_tp)
+    probs, base, lines = score(parts, keys, cache, meta, n_fsdp * n_tp)
     lines = lax.all_to_all(lines, ("fsdp", "tp"), 0, 0, tiled=True)
     attention = mix(probs, base, cache, steps)
     ratios, version_means = final(lines, rows, steps)
-    return (new_master, attention, ratios, version_means)
+    return (new_master, attention, ratios, version_means.reshape(VERSIONS))
 
 
 def solution(mesh):

time: 74.2 us -> 73.2 us (0.987)
  Pallas kernels: 23.7 us -> 22.6 us
    all_to_all x1, waiting for transfers between devices: 0.01 us -> 3.93 us  [shards(): weights = lax.all_to_all(fresh, 'tp', 0, 0, tiled=True).reshape(depth, -1)]
    ppermute x6, waiting for transfers between devices: 4.35 us -> 1 us  [move(): lax.ppermute(block, 'fsdp', [(i, i ^ hop) for i in range(n_fsdp)])]
  transfers between devices with their start and end apart: 8 -> 8, of which waited for: 3 -> 3; matrix products, arithmetic and copies ran while one was open for 0% -> 0% of each run, Pallas kernels for 24% -> 23%
where the time goes in v4:
time: 73.2 us; the launch traced here: 72.8 us
  starting transfers between devices  24.7 us (34%)
  Pallas kernels  22.6 us (31%)
  blocking collectives  14.7 us (20%)
  waiting for transfers between devices  9.95 us (14%)
  between operations  0.77 us (1%)
    all_to_all x1, blocking collectives, shards(): lax.all_to_all(partial.reshape(chips, tall, -1), 'fsdp', 0, 0, tiled=True...  14.7 us
    ppermute x6, starting transfers between devices, move(): lax.ppermute(block, 'fsdp', [(i, i ^ hop) for i in range(n_fsdp)])  10.9 us
    pallas_call x2, Pallas kernels, adam(): pl.pallas_call(adam_kernel, in_specs=[ANY] * 4, out_specs=ANY, out_shape=...  10.6 us
    all_to_all x1, starting transfers between devices, shards(): weights = lax.all_to_all(fresh, 'tp', 0, 0, tiled=True).reshape(depth, -1)  7.21 us
    all_to_all x1, starting transfers between devices, shards(): lines = lax.all_to_all(lines, ('fsdp', 'tp'), 0, 0, tiled=True)  6.61 us
    all_to_all x1, waiting for transfers between devices, shards(): lines = lax.all_to_all(lines, ('fsdp', 'tp'), 0, 0, tiled=True)  5.02 us
    pallas_call x1, Pallas kernels, mix(): pl.pallas_call(functools.partial(mix_kernel, steps), grid=(rows,), in_spe...  4.3 us
    all_to_all x1, waiting for transfers between devices, shards(): weights = lax.all_to_all(fresh, 'tp', 0, 0, tiled=True).reshape(depth, -1)  3.93 us
  transfers between devices with their start and end apart: 8, of which 3 were waited for; matrix products, arithmetic and copies ran while one was open for 0% of the time, Pallas kernels for 23%

profile of v4, /device:TPU:1, one launch (start us, length us, event | category | flops | bytes accessed | tf_op | source)
XLA Modules:
  0.0 72.8 jit_solution(3337420475777331237)
XLA Ops:
  0.6 1.0 %stage.1 = (f32[8,128]{1,0:T(8,128)S(1)}, bf16[16,16,512]{2,1,0:T(8,128)(2,1)S(1)}) custom-call(s32[4]{0:T(128)} %lengths.1, s32[4]{0:T(128)} %versions.1, f32[4,4]{1,0:T(4,128)} %recorded.1, bf16[4,4,8192]{2,1,0:T(4,128)(2,1)} %hidden.1), custom_call_target="tpu_custom_call" | custom-call | tf_op jit(solution)/shard_map/stage/pallas_call | solution.py:121
  1.7 2.1 %collective-permute-start = (bf16[4,2,16,512]{3,2,1,0:T(8,128)(2,1)S(1)}, bf16[4,2,16,512]{3,2,1,0:T(8,128)(2,1)S(1)}, u32[]{:S(2)}, u32[]{:S(2)}) collective-permute-start(bf16[4,2,16,512]{3,2,1,0:T(8,128)(2,1)S(1)} %bitcast.44), channel_id=1, source_target_pairs={{0,64},{8,72},{16,80},{24,88},{32,96},{40,104},{48,112},{56,120},{... | collective-permute-start | bytes 393224 | tf_op jit(solution)/shard_map/ppermute | solution.py:361
  3.8 5.1 %weights.1 = bf16[8,64,1280]{2,1,0:T(8,128)(2,1)} custom-call(f32[64,10240]{1,0:T(8,128)} %master.4, f32[64,10240]{1,0:T(8,128)} %moment.2, f32[64,10240]{1,0:T(8,128)} %second.2, bf16[64,10240]{1,0:T(8,128)(2,1)} %grad.2), custom_call_target="tpu_custom_call" | custom-call | flops 7864320 | bytes 11796480 | tf_op jit(solution)/shard_map/weights/pallas_call | solution.py:73
  9.0 0.0 collective-permute-done
  9.0 7.2 %all-to-all-start = ((bf16[8,64,1280]{2,1,0:T(8,128)(2,1)}), bf16[8,64,1280]{2,1,0:T(8,128)(2,1)S(1)}, u32[]{:S(2)}, u32[]{:S(2)}) async-start(bf16[8,64,1280]{2,1,0:T(8,128)(2,1)} %weights.1), calls=%async_computation | async-start | bytes 2621440 | tf_op jit(solution)/shard_map/all_to_all | solution.py:370
  16.2 2.8 %collective-permute-start.3 = (bf16[2,2,16,512]{3,2,0,1:T(8,128)(2,1)S(1)}, bf16[2,2,16,512]{3,2,0,1:T(8,128)(2,1)S(1)}, u32[]{:S(2)}, u32[]{:S(2)}) collective-permute-start(bf16[2,2,16,512]{3,2,0,1:T(8,128)(2,1)S(1)} %get-tuple-element.48), channel_id=1, source_target_pairs={{0,48},{8,56},{16,32},{24,40},{32,16},{40,24},{48,0},{56,8},{64,11... | collective-permute-start | bytes 196616 | tf_op jit(solution)/shard_map/ppermute | solution.py:361
  19.0 0.0 collective-permute-start.1
  19.0 1.3 %collective-permute-start.2 = (bf16[2,2,16,512]{3,2,0,1:T(8,128)(2,1)S(1)}, bf16[2,2,16,512]{3,2,0,1:T(8,128)(2,1)S(1)}, u32[]{:S(2)}, u32[]{:S(2)}) collective-permute-start(bf16[2,2,16,512]{3,2,0,1:T(8,128)(2,1)S(1)} %get-tuple-element.51), channel_id=1, source_target_pairs={{0,32},{8,40},{16,48},{24,56},{32,0},{40,8},{48,16},{56,24},{64,96... | collective-permute-start | bytes 196616 | tf_op jit(solution)/shard_map/ppermute | solution.py:361
  20.3 5.5 %master.3 = f32[64,10240]{1,0:T(8,128)} custom-call(f32[64,10240]{1,0:T(8,128)} %master.4, f32[64,10240]{1,0:T(8,128)} %moment.2, f32[64,10240]{1,0:T(8,128)} %second.2, bf16[64,10240]{1,0:T(8,128)(2,1)} %grad.2), custom_call_target="tpu_custom_call" | custom-call | flops 7864320 | bytes 11796480 | tf_op jit(solution)/shard_map/master/pallas_call | solution.py:73
  25.8 0.0 collective-permute-done.3
  25.9 0.0 collective-permute-done.1
  25.9 0.0 collective-permute-done.2
  25.9 2.0 %collective-permute-start.4 = (bf16[2,4,16,512]{3,2,1,0:T(8,128)(2,1)S(1)}, bf16[2,4,16,512]{3,2,1,0:T(8,128)(2,1)S(1)}, u32[]{:S(2)}, u32[]{:S(2)}) collective-permute-start(bf16[2,4,16,512]{3,2,1,0:T(8,128)(2,1)S(1)} %get-tuple-element.47), channel_id=1, source_target_pairs={{0,8},{8,0},{16,24},{24,16},{32,40},{40,32},{48,56},{56,48},{64,72... | collective-permute-start | bytes 393224 | tf_op jit(solution)/shard_map/ppermute | solution.py:361
  27.9 1.0 %collective-permute-done.4 = bf16[2,4,16,512]{3,2,1,0:T(8,128)(2,1)S(1)} collective-permute-done((bf16[2,4,16,512]{3,2,1,0:T(8,128)(2,1)S(1)}, bf16[2,4,16,512]{3,2,1,0:T(8,128)(2,1)S(1)}, u32[]{:S(2)}, u32[]{:S(2)}) %collective-permute-start.4) | collective-permute-done | bytes 131104 | tf_op jit(solution)/shard_map/ppermute | solution.py:361
  29.0 3.9 %all-to-all-done = bf16[8,64,1280]{2,1,0:T(8,128)(2,1)S(1)} async-done(((bf16[8,64,1280]{2,1,0:T(8,128)(2,1)}), bf16[8,64,1280]{2,1,0:T(8,128)(2,1)S(1)}, u32[]{:S(2)}, u32[]{:S(2)}) %all-to-all-start) | async-done | bytes 1310752 | tf_op jit(solution)/shard_map/all_to_all | solution.py:370
  32.9 0.4 product.3
  33.3 2.6 %collective-permute-start.5 = (f32[128,1280]{1,0:T(8,128)S(1)}, f32[128,1280]{1,0:T(8,128)S(1)}, u32[]{:S(2)}, u32[]{:S(2)}) collective-permute-start(f32[128,1280]{1,0:T(8,128)S(1)} %product.3), channel_id=1, source_target_pairs={{0,8},{8,0},{16,24},{24,16},{32,40},{40,32},{48,56},{56,48},{64,72... | collective-permute-start | bytes 1966088 | tf_op jit(solution)/shard_map/ppermute | solution.py:361
  35.9 2.1 %product.2 = (f32[128,1280]{1,0:T(8,128)S(1)}, bf16[3,4096,128]{2,1,0:T(8,128)(2,1)S(1)}) custom-call(bf16[16,16,512]{2,1,0:T(8,128)(2,1)S(1)} %bitcast.38, bf16[512,1280]{1,0:T(8,128)(2,1)S(1)} %bitcast.36, bf16[4,1,2,4096,128]{4,3,2,1,0:T(8,128)(2,1)} %values.1), custom_call_target="tpu_custom_call" | custom-call | flops 167772160 | bytes 2097152 | tf_op jit(solution)/shard_map/product/pallas_call | solution.py:179
  38.1 0.0 collective-permute-done.5
  38.1 0.1 add.3
  38.1 14.7 %all_to_all.21.parts = f32[8,16,1280]{2,1,0:T(8,128)S(1)} all-to-all(f32[8,16,1280]{2,1,0:T(8,128)S(1)} %bitcast.40), channel_id=1, replica_groups={{0,16,32,48,64,80,96,112},{8,24,40,56,72,88,104,120},{1,17,33,49,65,81,..., dimensions={0} | all-to-all | bytes 1310720 | tf_op jit(solution)/shard_map/all_to_all | solution.py:384
  52.8 3.1 %score.1 = (bf16[4,32,4096]{2,1,0:T(8,128)(2,1)S(1)}, f32[4,32,128]{2,1,0:T(8,128)S(1)}, f32[128,128]{1,0:T(8,128)}) custom-call(f32[8,16,1280]{2,1,0:T(8,128)S(1)} %all_to_all.21.parts, bf16[3,4096,128]{2,1,0:T(8,128)(2,1)S(1)} %get-tuple-element.39.keys, bf16[4,1,2,4096,128]{4,3,2,1,0:T(8,128)(2,1)} %values.1, f32[8,128]{1,0:T(8,128)S(1)} %get-tuple-element.40.meta), custom_call_target="tpu_custom_call" | custom-call | flops 134217728 | bytes 4194304 | tf_op jit(solution)/shard_map/score/pallas_call | solution.py:251
  56.0 6.6 %all-to-all-start.2 = ((f32[128,1,128]{2,1,0:T(1,128)}), f32[128,1,128]{2,1,0:T(1,128)S(1)}, u32[]{:S(2)}, u32[]{:S(2)}) async-start(f32[128,1,128]{2,1,0:T(1,128)} %bitcast.22), calls=%async_computation.2 | async-start | bytes 131072 | tf_op jit(solution)/shard_map/all_to_all | solution.py:388
  62.6 4.3 %mix.1 = bf16[4,4,1024]{2,1,0:T(4,128)(2,1)} custom-call(bf16[4,32,4096]{2,1,0:T(8,128)(2,1)S(1)} %get-tuple-element.41.probs, f32[4,32,128]{2,1,0:T(8,128)S(1)} %get-tuple-element.42.base, bf16[4,1,2,4096,128]{4,3,2,1,0:T(8,128)(2,1)} %values.1), custom_call_target="tpu_custom_call" | custom-call | flops 134217728 | bytes 4194304 | tf_op jit(solution)/shard_map/mix/pallas_call | solution.py:288
  66.9 5.0 %all-to-all-done.2 = f32[128,1,128]{2,1,0:T(1,128)S(1)} async-done(((f32[128,1,128]{2,1,0:T(1,128)}), f32[128,1,128]{2,1,0:T(1,128)S(1)}, u32[]{:S(2)}, u32[]{:S(2)}) %all-to-all-start.2) | async-done | bytes 65568 | tf_op jit(solution)/shard_map/all_to_all | solution.py:388
  71.9 0.9 %ratios.1 = (f32[4,4]{1,0:T(4,128)}, f32[1,4]{1,0:T(1,128)}) custom-call(f32[128,128]{1,0:T(8,128)S(1)} %bitcast.39), custom_call_target="tpu_custom_call" | custom-call | tf_op jit(solution)/shard_map/ratios/pallas_call | solution.py:339
  (5 shorter events, 0.1 us)
Async XLA Ops:
  1.7 7.3 %collective-permute-start = (bf16[4,2,16,512]{3,2,1,0:T(8,128)(2,1)S(1)}, bf16[4,2,16,512]{3,2,1,0:T(8,128)(2,1)S(1)}, u32[]{:S(2)}, u32[]{:S(2)}) collective-permute-start(bf16[4,2,16,512]{3,2,1,0:T(8,128)(2,1)S(1)} %bitcast.44), channel_id=1, source_target_pairs={{0,64},{8,72},{16,80},{24,88},{32,96},{40,104},{48,112},{56,120},{... | collective-permute-start | bytes 393224 | tf_op jit(solution)/shard_map/ppermute | solution.py:361
  9.0 23.9 %all-to-all-start = ((bf16[8,64,1280]{2,1,0:T(8,128)(2,1)}), bf16[8,64,1280]{2,1,0:T(8,128)(2,1)S(1)}, u32[]{:S(2)}, u32[]{:S(2)}) async-start(bf16[8,64,1280]{2,1,0:T(8,128)(2,1)} %weights.1), calls=%async_computation | async-start | bytes 2621440 | tf_op jit(solution)/shard_map/all_to_all | solution.py:370
  16.2 9.6 %collective-permute-start.3 = (bf16[2,2,16,512]{3,2,0,1:T(8,128)(2,1)S(1)}, bf16[2,2,16,512]{3,2,0,1:T(8,128)(2,1)S(1)}, u32[]{:S(2)}, u32[]{:S(2)}) collective-permute-start(bf16[2,2,16,512]{3,2,0,1:T(8,128)(2,1)S(1)} %get-tuple-element.48), channel_id=1, source_target_pairs={{0,48},{8,56},{16,32},{24,40},{32,16},{40,24},{48,0},{56,8},{64,11... | collective-permute-start | bytes 196616 | tf_op jit(solution)/shard_map/ppermute | solution.py:361
  19.0 6.8 %collective-permute-start.1 = (bf16[2,2,16,512]{3,2,0,1:T(8,128)(2,1)S(1)}, bf16[2,2,16,512]{3,2,0,1:T(8,128)(2,1)S(1)}, u32[]{:S(2)}, u32[]{:S(2)}) collective-permute-start(bf16[2,2,16,512]{3,2,0,1:T(8,128)(2,1)S(1)} %get-tuple-element.50), channel_id=1, source_target_pairs={{0,16},{8,24},{16,0},{24,8},{32,48},{40,56},{48,32},{56,40},{64,80... | collective-permute-start | bytes 196616 | tf_op jit(solution)/shard_map/ppermute | solution.py:361
  19.0 6.8 %collective-permute-start.2 = (bf16[2,2,16,512]{3,2,0,1:T(8,128)(2,1)S(1)}, bf16[2,2,16,512]{3,2,0,1:T(8,128)(2,1)S(1)}, u32[]{:S(2)}, u32[]{:S(2)}) collective-permute-start(bf16[2,2,16,512]{3,2,0,1:T(8,128)(2,1)S(1)} %get-tuple-element.51), channel_id=1, source_target_pairs={{0,32},{8,40},{16,48},{24,56},{32,0},{40,8},{48,16},{56,24},{64,96... | collective-permute-start | bytes 196616 | tf_op jit(solution)/shard_map/ppermute | solution.py:361
  25.9 3.0 %collective-permute-start.4 = (bf16[2,4,16,512]{3,2,1,0:T(8,128)(2,1)S(1)}, bf16[2,4,16,512]{3,2,1,0:T(8,128)(2,1)S(1)}, u32[]{:S(2)}, u32[]{:S(2)}) collective-permute-start(bf16[2,4,16,512]{3,2,1,0:T(8,128)(2,1)S(1)} %get-tuple-element.47), channel_id=1, source_target_pairs={{0,8},{8,0},{16,24},{24,16},{32,40},{40,32},{48,56},{56,48},{64,72... | collective-permute-start | bytes 393224 | tf_op jit(solution)/shard_map/ppermute | solution.py:361
  33.3 4.8 %collective-permute-start.5 = (f32[128,1280]{1,0:T(8,128)S(1)}, f32[128,1280]{1,0:T(8,128)S(1)}, u32[]{:S(2)}, u32[]{:S(2)}) collective-permute-start(f32[128,1280]{1,0:T(8,128)S(1)} %product.3), channel_id=1, source_target_pairs={{0,8},{8,0},{16,24},{24,16},{32,40},{40,32},{48,56},{56,48},{64,72... | collective-permute-start | bytes 1966088 | tf_op jit(solution)/shard_map/ppermute | solution.py:361
  56.0 15.9 %all-to-all-start.2 = ((f32[128,1,128]{2,1,0:T(1,128)}), f32[128,1,128]{2,1,0:T(1,128)S(1)}, u32[]{:S(2)}, u32[]{:S(2)}) async-start(f32[128,1,128]{2,1,0:T(1,128)} %bitcast.22), calls=%async_computation.2 | async-start | bytes 131072 | tf_op jit(solution)/shard_map/all_to_all | solution.py:388
